TPU v7x, 32 devices: a whole 2x2x4 slice. The times are simulated.
32 devices in a mesh: dp: 4 (over x, core), expert: 4 (over z), tensor: 2 (over y).
Axes of the slice: x: 2, y: 2, z: 4, core: 2. Of those that a mesh axis runs over, the one named last changes fastest.
Arguments:
- x_in: bfloat16 [4096, 1536], P(('dp', 'expert')), may hold values from -6 to 6
- segments: int32 [4096], P('dp'), may hold values from 0 to 1023, as said below
- chosen: int32 [4096, 8], P(('dp', 'expert')), may hold values from 0 to 39, all different within a row; in each aligned block of 256 rows (0 to 255, 256 to 511, ...) at most 80 rows name the same one
- out_grad: bfloat16 [4096, 1536], P(('dp', 'expert')), may hold values from -6 to 6
- norm1_gain: float32 [1536], replicated, may hold values from 0.5 to 1.5
- w_query: bfloat16 [1536, 1536], P(None, 'tensor'), may hold values from -0.3125 to 0.3125
- w_key: bfloat16 [1536, 512], P(None, 'tensor'), may hold values from -0.15625 to 0.15625
- w_value: bfloat16 [1536, 512], P(None, 'tensor'), may hold values from -0.15625 to 0.15625
- w_out: bfloat16 [1536, 1536], P('tensor'), may hold values from -0.625 to 0.625
- norm2_gain: float32 [1536], replicated, may hold values from 0.5 to 1.5
- w_router: bfloat16 [1536, 40], replicated, may hold values from -0.078125 to 0.078125
- w_gate: bfloat16 [40, 1536, 512], P('expert', None, 'tensor'), may hold values from -0.15625 to 0.15625
- w_up: bfloat16 [40, 1536, 512], P('expert', None, 'tensor'), may hold values from -0.15625 to 0.15625
- w_down: bfloat16 [40, 512, 1536], P('expert', 'tensor'), may hold values from -1 to 1
Outputs:
- block_out: bfloat16 [4096, 1536], P(('dp', 'expert'), 'tensor')
- input_grad: float32 [4096, 1536], P(('dp', 'expert'))
- grad_norm1: float32 [1536], P(('dp', 'expert'))
- grad_query: float32 [1536, 1536], P(('dp', 'expert'), 'tensor')
- grad_key: float32 [1536, 512], P(('dp', 'expert'), 'tensor')
- grad_value: float32 [1536, 512], P(('dp', 'expert'), 'tensor')
- grad_out: float32 [1536, 1536], P('tensor', ('dp', 'expert'))
- grad_norm2: float32 [1536], P(('dp', 'expert'))
- grad_router: float32 [1536, 40], P(('dp', 'expert'))
- grad_gate: float32 [40, 1536, 512], P('expert', 'dp', 'tensor')
- grad_up: float32 [40, 1536, 512], P('expert', 'dp', 'tensor')
- grad_down: float32 [40, 512, 1536], P('expert', 'tensor', 'dp')
Inputs may be any that keep to these rules, and one draw needn't show every extreme that they name: `segments`: document numbers never fall along a sequence, and the last token of every sequence carries 1024 - 1; documents do not attend to each other. `chosen`: each token names 8 different experts; among the tokens of one device no expert is named by more than 80 of them.
All inputs are finite; a program needn't handle non-finite values.
Results may differ from a plain program's by a relative error of at most 0.022.
Values may be sent and summed in bfloat16 or wider, within the bound.
No kernel may reach another device: no remote copies, remote signals or barrier semaphores. Data moves between devices by JAX's collectives and lax.ppermute only.
A program may use at most 320 MiB of HBM per device.

v0:
```python
import jax
import jax.numpy as jnp
from jax import lax
from jax.sharding import PartitionSpec as P

HEAD_DIM = 64


EPSILON = 1e-05
ROPE_BASE = 10000.0
MASKED = -1e30


def rotate(values, positions, direction):
    head_size = values.shape[-1]
    half_dim = head_size // 2
    inverse = ROPE_BASE ** (-2.0 * jnp.arange(half_dim, dtype=jnp.float32) / head_size)
    angles = positions.astype(jnp.float32)[:, None] * inverse[None, :]
    cosine = jnp.cos(angles)[:, None, :]
    sine = direction * jnp.sin(angles)[:, None, :]
    first_half = values[..., :half_dim]
    second_half = values[..., half_dim:]
    return jnp.concatenate(
        [first_half * cosine - second_half * sine, second_half * cosine + first_half * sine],
        axis=-1,
    )


def norm_forward(values, gain):
    norm_scale = lax.rsqrt(jnp.mean(values * values, axis=1, keepdims=True) + EPSILON)
    return (norm_scale, values * norm_scale * gain)


def norm_backward(values, norm_scale, gain, grad_normed):
    weighted = grad_normed * gain
    inner = jnp.mean(weighted * values, axis=1, keepdims=True)
    grad_values = norm_scale * weighted - values * (norm_scale * norm_scale * norm_scale) * inner
    grad_gain = jnp.sum(grad_normed * values * norm_scale, axis=0)
    return (grad_values, grad_gain)


def body(
    x_in,
    segments,
    chosen,
    out_grad,
    norm1_gain,
    w_query,
    w_key,
    w_value,
    w_out,
    norm2_gain,
    w_router,
    w_gate,
    w_up,
    w_down,
):
    tok_rows, full_width = x_in.shape
    head_size = HEAD_DIM
    kv_local = w_key.shape[1] // head_size
    query_local = w_query.shape[1] // head_size
    groups = query_local // kv_local
    experts_local = w_gate.shape[0]
    expert_devices = lax.axis_size("expert")
    tensor_devices = lax.axis_size("tensor")
    total_experts = experts_local * expert_devices
    top_count = chosen.shape[1]
    capacity = tok_rows * top_count * 25 // (16 * total_experts)
    half_width = full_width // tensor_devices
    column_start = lax.axis_index("tensor") * half_width
    row_start = lax.axis_index("expert") * tok_rows
    seq_length = segments.shape[0]
    positions = row_start + jnp.arange(tok_rows, dtype=jnp.int32)
    key_positions = jnp.arange(seq_length, dtype=jnp.int32)
    query_segments = lax.dynamic_slice_in_dim(segments, row_start, tok_rows)
    key_mask = (query_segments[:, None] == segments[None, :]) & (
        positions[:, None] >= key_positions[None, :]
    )
    score_scale = head_size ** (-0.5)
    inputs = x_in.astype(jnp.float32)
    scale_one, normed_one = norm_forward(inputs, norm1_gain)
    normed_one = normed_one.astype(jnp.bfloat16)
    query_pre = jnp.dot(normed_one, w_query, preferred_element_type=jnp.float32)
    key_pre = jnp.dot(normed_one, w_key, preferred_element_type=jnp.float32)
    value_pre = jnp.dot(normed_one, w_value, preferred_element_type=jnp.float32)
    query_rot = rotate(query_pre.reshape(tok_rows, query_local, head_size), positions, 1.0).astype(
        jnp.bfloat16
    )
    key_rot = (
        rotate(key_pre.reshape(tok_rows, kv_local, head_size), positions, 1.0)
        .astype(jnp.bfloat16)
        .reshape(tok_rows, kv_local * head_size)
    )
    value_low = value_pre.astype(jnp.bfloat16)
    keys_all, values_all = (
        lax.all_gather(key_rot, "expert", axis=0, tiled=True),
        lax.all_gather(value_low, "expert", axis=0, tiled=True),
    )
    query_heads = query_rot.reshape(tok_rows, kv_local, groups, head_size).transpose(1, 0, 2, 3)
    key_heads = keys_all.reshape(seq_length, kv_local, head_size).transpose(1, 0, 2)
    value_heads = values_all.reshape(seq_length, kv_local, head_size).transpose(1, 0, 2)

    def head_forward(operands):
        q_head, k_head, v_head = operands
        scores = (
            jnp.einsum("qgd,kd->gqk", q_head, k_head, preferred_element_type=jnp.float32)
            * score_scale
        )
        scores = jnp.where(key_mask[None], scores, MASKED)
        row_peak = jnp.max(scores, axis=2, keepdims=True)
        raw_weights = jnp.exp(scores - row_peak)
        row_total = jnp.sum(raw_weights, axis=2, keepdims=True)
        probs_low = (raw_weights / row_total).astype(jnp.bfloat16)
        head_out = jnp.einsum("gqk,kd->qgd", probs_low, v_head, preferred_element_type=jnp.float32)
        return (head_out, (row_peak + jnp.log(row_total))[:, :, 0])

    attended_heads, log_totals = lax.map(head_forward, (query_heads, key_heads, value_heads))
    attended_low = (
        attended_heads.transpose(1, 0, 2, 3)
        .reshape(tok_rows, query_local * head_size)
        .astype(jnp.bfloat16)
    )
    head_partial = jnp.dot(attended_low, w_out, preferred_element_type=jnp.float32)
    hidden_one = inputs + lax.psum(head_partial.astype(jnp.bfloat16), "tensor").astype(jnp.float32)
    scale_two, normed_two = norm_forward(hidden_one, norm2_gain)
    normed_two = normed_two.astype(jnp.bfloat16)
    logits = jnp.dot(normed_two, w_router, preferred_element_type=jnp.float32)
    expert_hot = (chosen[:, :, None] == jnp.arange(total_experts, dtype=jnp.int32)).astype(
        jnp.float32
    )
    picked = jnp.sum(expert_hot * logits[:, None, :], axis=2)
    gate_weights = jax.nn.softmax(picked, axis=1)
    flat_expert = chosen.reshape(-1)
    flat_hot = (flat_expert[:, None] == jnp.arange(total_experts, dtype=jnp.int32)).astype(
        jnp.int32
    )
    slot_index = jnp.sum(jnp.cumsum(flat_hot, axis=0) * flat_hot, axis=1) - 1
    dest_index = flat_expert * capacity + slot_index
    dispatched = (
        jnp.zeros((total_experts * capacity, full_width), jnp.bfloat16)
        .at[dest_index]
        .set(jnp.repeat(normed_two, top_count, axis=0))
        .reshape(total_experts, capacity, full_width)
    )
    received = lax.all_to_all(dispatched, "expert", split_axis=0, concat_axis=0, tiled=True)
    slot_count = received.shape[1]
    expert_slot_count = received.shape[1]
    grouped = received.reshape(expert_devices, experts_local, expert_slot_count, full_width)
    gate_pre = jnp.einsum("secd,edf->secf", grouped, w_gate, preferred_element_type=jnp.float32)
    up_pre = jnp.einsum("secd,edf->secf", grouped, w_up, preferred_element_type=jnp.float32)
    activated = (jax.nn.silu(gate_pre) * up_pre).astype(jnp.bfloat16)
    summed_out = lax.psum_scatter(
        jnp.einsum("secf,efd->secd", activated, w_down, preferred_element_type=jnp.float32).astype(
            jnp.bfloat16
        ),
        "tensor",
        scatter_dimension=3,
        tiled=True,
    ).astype(jnp.float32)
    sent_back = lax.all_to_all(
        summed_out.reshape(total_experts, slot_count, half_width).astype(jnp.bfloat16),
        "expert",
        split_axis=0,
        concat_axis=0,
        tiled=True,
    ).astype(jnp.float32)
    out_cot = out_grad.astype(jnp.float32)
    cot_half = lax.dynamic_slice_in_dim(out_cot, column_start, half_width, 1)
    residual_half = lax.dynamic_slice_in_dim(hidden_one, column_start, half_width, 1)
    mixed_rows = sent_back.reshape(total_experts * capacity, half_width)[dest_index].reshape(
        tok_rows, top_count, half_width
    )
    mixture_half = jnp.sum(gate_weights[:, :, None] * mixed_rows, axis=1)
    gate_local = jnp.sum(mixed_rows * cot_half[:, None, :], axis=2)
    block_out = (residual_half + mixture_half).astype(jnp.bfloat16)
    gate_grads = lax.psum(gate_local, "tensor")
    picked_grads = gate_weights * (
        gate_grads - jnp.sum(gate_weights * gate_grads, axis=1, keepdims=True)
    )
    logit_grads = jnp.sum(expert_hot * picked_grads[:, :, None], axis=1).astype(jnp.bfloat16)
    grad_router = jnp.einsum(
        "rd,re->de", normed_two, logit_grads, preferred_element_type=jnp.float32
    )
    normed_two_grad = jnp.einsum(
        "re,de->rd", logit_grads, w_router, preferred_element_type=jnp.float32
    )
    row_cots = (
        (gate_weights[:, :, None] * out_cot[:, None, :])
        .astype(jnp.bfloat16)
        .reshape(tok_rows * top_count, full_width)
    )
    cot_buffer = (
        jnp.zeros((total_experts * capacity, full_width), jnp.bfloat16)
        .at[dest_index]
        .set(row_cots)
        .reshape(total_experts, capacity, full_width)
    )
    cot_received = lax.all_to_all(cot_buffer, "expert", split_axis=0, concat_axis=0, tiled=True)
    grouped_in = received.reshape(expert_devices, experts_local, capacity, full_width)
    grouped_cot = cot_received.reshape(expert_devices, experts_local, capacity, full_width)
    gate_again = jnp.einsum(
        "secd,edf->secf", grouped_in, w_gate, preferred_element_type=jnp.float32
    )
    up_again = jnp.einsum("secd,edf->secf", grouped_in, w_up, preferred_element_type=jnp.float32)
    sigmoid_gate = jax.nn.sigmoid(gate_again)
    swish_gate = gate_again * sigmoid_gate
    activated_again = (swish_gate * up_again).astype(jnp.bfloat16)
    grad_down = jnp.einsum(
        "secf,secd->efd", activated_again, grouped_cot, preferred_element_type=jnp.float32
    )
    activated_grad = jnp.einsum(
        "secd,efd->secf", grouped_cot, w_down, preferred_element_type=jnp.float32
    )
    gate_pre_grad = (
        activated_grad * up_again * sigmoid_gate * (1.0 + gate_again * (1.0 - sigmoid_gate))
    ).astype(jnp.bfloat16)
    up_pre_grad = (activated_grad * swish_gate).astype(jnp.bfloat16)
    grad_gate = jnp.einsum(
        "secd,secf->edf", grouped_in, gate_pre_grad, preferred_element_type=jnp.float32
    )
    grad_up = jnp.einsum(
        "secd,secf->edf", grouped_in, up_pre_grad, preferred_element_type=jnp.float32
    )
    partial_in_grad = jnp.einsum(
        "secf,edf->secd", gate_pre_grad, w_gate, preferred_element_type=jnp.float32
    ) + jnp.einsum("secf,edf->secd", up_pre_grad, w_up, preferred_element_type=jnp.float32)
    in_grad_half = lax.psum_scatter(
        partial_in_grad.astype(jnp.bfloat16), "tensor", scatter_dimension=3, tiled=True
    ).astype(jnp.float32)
    grad_back = lax.all_to_all(
        in_grad_half.reshape(total_experts, capacity, half_width).astype(jnp.bfloat16),
        "expert",
        split_axis=0,
        concat_axis=0,
        tiled=True,
    ).astype(jnp.float32)
    back_rows = grad_back.reshape(total_experts * capacity, half_width)[dest_index].reshape(
        tok_rows, top_count, half_width
    )
    expert_grad = lax.all_gather(
        jnp.sum(back_rows, axis=1).astype(jnp.bfloat16), "tensor", axis=1, tiled=True
    ).astype(jnp.float32)
    normed_two_grad = normed_two_grad + expert_grad
    hidden_grad, gain_two_grad = norm_backward(hidden_one, scale_two, norm2_gain, normed_two_grad)
    hidden_grad = hidden_grad + out_cot
    branch_cot = hidden_grad.astype(jnp.bfloat16)
    grad_out = jnp.einsum("rh,rd->hd", attended_low, branch_cot, preferred_element_type=jnp.float32)
    attended_grad = jnp.einsum(
        "rd,hd->rh", branch_cot, w_out, preferred_element_type=jnp.float32
    ).astype(jnp.bfloat16)
    grad_heads = attended_grad.reshape(tok_rows, kv_local, groups, head_size).transpose(1, 0, 2, 3)

    def head_backward(operands):
        q_head, k_head, v_head, d_head, o_head, lse_head = operands
        scores = (
            jnp.einsum("qgd,kd->gqk", q_head, k_head, preferred_element_type=jnp.float32)
            * score_scale
        )
        scores = jnp.where(key_mask[None], scores, MASKED)
        attention_probs = jnp.exp(scores - lse_head[:, :, None])
        probs_low = attention_probs.astype(jnp.bfloat16)
        value_part = jnp.einsum(
            "gqk,qgd->kd", probs_low, d_head, preferred_element_type=jnp.float32
        )
        probs_grad = jnp.einsum("qgd,kd->gqk", d_head, v_head, preferred_element_type=jnp.float32)
        delta_rows = jnp.sum(d_head.astype(jnp.float32) * o_head, axis=2).transpose(1, 0)
        scores_grad = (attention_probs * (probs_grad - delta_rows[:, :, None])).astype(jnp.bfloat16)
        query_part = (
            jnp.einsum("gqk,kd->qgd", scores_grad, k_head, preferred_element_type=jnp.float32)
            * score_scale
        )
        key_part = (
            jnp.einsum("gqk,qgd->kd", scores_grad, q_head, preferred_element_type=jnp.float32)
            * score_scale
        )
        return (query_part, key_part, value_part)

    query_grads, key_grads_all, value_grads_all = lax.map(
        head_backward, (query_heads, key_heads, value_heads, grad_heads, attended_heads, log_totals)
    )
    key_grad_rows = key_grads_all.transpose(1, 0, 2).reshape(seq_length, kv_local * head_size)
    value_grad_rows = value_grads_all.transpose(1, 0, 2).reshape(seq_length, kv_local * head_size)
    key_grad_own, value_grad_own = (
        lax.psum_scatter(
            key_grad_rows.astype(jnp.bfloat16), "expert", scatter_dimension=0, tiled=True
        ).astype(jnp.float32),
        lax.psum_scatter(
            value_grad_rows.astype(jnp.bfloat16), "expert", scatter_dimension=0, tiled=True
        ).astype(jnp.float32),
    )
    query_grad = (
        rotate(
            query_grads.transpose(1, 0, 2, 3).reshape(tok_rows, query_local, head_size),
            positions,
            -1.0,
        )
        .astype(jnp.bfloat16)
        .reshape(tok_rows, query_local * head_size)
    )
    key_grad = (
        rotate(key_grad_own.reshape(tok_rows, kv_local, head_size), positions, -1.0)
        .astype(jnp.bfloat16)
        .reshape(tok_rows, kv_local * head_size)
    )
    value_grad = value_grad_own.astype(jnp.bfloat16)
    grad_query = jnp.einsum("rd,rh->dh", normed_one, query_grad, preferred_element_type=jnp.float32)
    grad_key = jnp.einsum("rd,rh->dh", normed_one, key_grad, preferred_element_type=jnp.float32)
    grad_value = jnp.einsum("rd,rh->dh", normed_one, value_grad, preferred_element_type=jnp.float32)
    normed_one_partial = jnp.einsum(
        "rh,dh->rd", query_grad, w_query, preferred_element_type=jnp.float32
    )
    normed_one_partial = normed_one_partial + jnp.einsum(
        "rh,dh->rd", key_grad, w_key, preferred_element_type=jnp.float32
    )
    normed_one_partial = normed_one_partial + jnp.einsum(
        "rh,dh->rd", value_grad, w_value, preferred_element_type=jnp.float32
    )
    normed_one_grad = lax.psum(normed_one_partial.astype(jnp.bfloat16), "tensor").astype(
        jnp.float32
    )
    input_part, gain_one_grad = norm_backward(inputs, scale_one, norm1_gain, normed_one_grad)
    input_grad = hidden_grad + input_part
    dense_sums = (
        lax.psum_scatter(grad_query, ("dp", "expert"), scatter_dimension=0, tiled=True),
        lax.psum_scatter(grad_key, ("dp", "expert"), scatter_dimension=0, tiled=True),
        lax.psum_scatter(grad_value, ("dp", "expert"), scatter_dimension=0, tiled=True),
        lax.psum_scatter(grad_out, ("dp", "expert"), scatter_dimension=1, tiled=True),
        lax.psum_scatter(grad_router, ("dp", "expert"), scatter_dimension=0, tiled=True),
        lax.psum_scatter(gain_one_grad, ("dp", "expert"), scatter_dimension=0, tiled=True),
        lax.psum_scatter(gain_two_grad, ("dp", "expert"), scatter_dimension=0, tiled=True),
    )
    expert_sums = (
        lax.psum_scatter(
            grad_gate.astype(jnp.bfloat16), "dp", scatter_dimension=1, tiled=True
        ).astype(jnp.float32),
        lax.psum_scatter(
            grad_up.astype(jnp.bfloat16), "dp", scatter_dimension=1, tiled=True
        ).astype(jnp.float32),
        lax.psum_scatter(
            grad_down.astype(jnp.bfloat16), "dp", scatter_dimension=2, tiled=True
        ).astype(jnp.float32),
    )
    return (
        block_out,
        input_grad,
        dense_sums[5],
        dense_sums[0],
        dense_sums[1],
        dense_sums[2],
        dense_sums[3],
        dense_sums[6],
        dense_sums[4],
        expert_sums[0],
        expert_sums[1],
        expert_sums[2],
    )


def solution(mesh):
    return jax.shard_map(
        body,
        mesh=mesh,
        in_specs=(
            P(("dp", "expert"), None),
            P("dp"),
            P(("dp", "expert"), None),
            P(("dp", "expert"), None),
            P(),
            P(None, "tensor"),
            P(None, "tensor"),
            P(None, "tensor"),
            P("tensor", None),
            P(),
            P(),
            P("expert", None, "tensor"),
            P("expert", None, "tensor"),
            P("expert", "tensor", None),
        ),
        out_specs=(
            P(("dp", "expert"), "tensor"),
            P(("dp", "expert"), None),
            P(("dp", "expert")),
            P(("dp", "expert"), "tensor"),
            P(("dp", "expert"), "tensor"),
            P(("dp", "expert"), "tensor"),
            P("tensor", ("dp", "expert")),
            P(("dp", "expert")),
            P(("dp", "expert"), None),
            P("expert", "dp", "tensor"),
            P("expert", "dp", "tensor"),
            P("expert", "tensor", "dp"),
        ),
        check_vma=False,
    )
```

profile of v0, /device:TPU:0, one launch (start us, length us, event | category | flops | bytes accessed | tf_op | source)
XLA Modules:
  0.0 1683.1 jit_solution(232387086112431005)
XLA Ops:
  13.2 18.0 %all_gather.10 = bf16[1024,256]{0,1:T(8,128)(2,1)} all-gather(bf16[256,256]{0,1:T(8,128)(2,1)S(1)} %bitcast.373), channel_id=1, replica_groups=mesh['dp'=4,'expert'=4,'tensor'=2] {'expert'}, dimensions={0}, use_global_device_ids=true | all-gather | bytes 655360 | tf_op jit(solution)/shard_map/all_gather | solution.py:96
  31.2 17.2 %all_gather.9 = bf16[1024,256]{1,0:T(8,128)(2,1)} all-gather(bf16[256,256]{1,0:T(8,128)(2,1)S(1)} %convolution_convert_fusion.3), channel_id=1, replica_groups=mesh['dp'=4,'expert'=4,'tensor'=2] {'expert'}, dimensions={0}, use_global_device_ids=true | all-gather | bytes 655360 | tf_op jit(solution)/shard_map/all_gather | solution.py:97
  56.8 26.1 %while.28 = (s32[]{:T(128)}, f32[4,256,3,64]{1,3,2,0:T(8,128)}, f32[4,3,256]{2,1,0:T(4,128)}, bf16[4,1024,64]{1,2,0:T(8,128)(2,1)}, bf16[4,1024,64]{1,2,0:T(8,12...) while((s32[]{:T(128)}, f32[4,256,3,64]{1,3,2,0:T(8,128)}, ...), condition=%wide.region_4.5_spmd.clone, body=%wide.region_1.4_spmd.clone.sunk | while | flops 211549440 | bytes 11076721 | solution.py:117
  95.9 22.0 %reduce-window.6 = s32[40,16,128]{2,1,0:T(8,128)} reduce-window(s32[40,16,128]{2,1,0:T(8,128)} %fusion.122, s32[]{:T(128)} %copy.192), window={size=1x1x128 pad=0_0x0_0x127_0}, to_apply=%region_10.11 | reduce-window | flops 10403840 | bytes 655364 | tf_op jit(solution)/shard_map/reduce-window
  126.6 16.1 scatter_custom_fusion
  152.0 16.5 scatter_custom_fusion.1
  168.5 194.0 %all-to-all-done = bf16[40,80,1536]{2,1,0:T(8,128)(2,1)} async-done(((bf16[40,80,1536]{2,1,0:T(8,128)(2,1)}), bf16[40,80,1536]{2,1,0:T(8,128)(2,1)}, u32[]{:S(2)}, u32[]{:S(2)}) %all-to-all-start) | async-done | bytes 9830432 | tf_op jit(solution)/shard_map/all_to_all | solution.py:145
  389.7 192.1 %all-to-all-done.2 = bf16[40,80,1536]{2,1,0:T(8,128)(2,1)} async-done(((bf16[40,80,1536]{2,1,0:T(8,128)(2,1)}), bf16[40,80,1536]{2,1,0:T(8,128)(2,1)}, u32[]{:S(2)}, u32[]{:S(2)}) %all-to-all-start.2) | async-done | bytes 9830432 | tf_op jit(solution)/shard_map/all_to_all | solution.py:198
  617.4 15.6 fusion.65
  633.0 84.1 %reduce-scatter.17.cloned.1.call-done = bf16[4,10,80,768]{3,2,0,1:T(8,128)(2,1)} async-done(((bf16[4,10,80,1536]{3,2,0,1:T(8,128)(2,1)}), bf16[4,10,80,768]{3,2,0,1:T(8,128)(2,1)}) %reduce-scatter.17.cloned.1.call-update) | async-done | bytes 4915216 | tf_op jit(solution)/shard_map/reduce_scatter | solution.py:152
  727.1 107.1 %reduce-scatter.19.cloned.1.call-done = bf16[4,10,80,768]{3,2,0,1:T(8,128)(2,1)} async-done(((bf16[4,10,80,1536]{3,2,0,1:T(8,128)(2,1)}), bf16[4,10,80,768]{3,2,0,1:T(8,128)(2,1)}) %reduce-scatter.19.cloned.1.call-update) | async-done | bytes 4915216 | tf_op jit(solution)/shard_map/reduce_scatter | solution.py:227
  852.5 14.5 gather_fusion
  878.8 74.3 %all-to-all-done.3 = bf16[40,80,768]{2,1,0:T(8,128)(2,1)} async-done(((bf16[40,80,768]{2,1,0:T(8,128)(2,1)}), bf16[40,80,768]{2,1,0:T(8,128)(2,1)}, u32[]{:S(2)}, u32[]{:S(2)}) %all-to-all-start.3) | async-done | bytes 4915232 | tf_op jit(solution)/shard_map/all_to_all | solution.py:230
  999.1 41.0 %while.29 = (s32[]{:T(128)}, f32[4,256,3,64]{1,3,2,0:T(8,128)}, bf16[4,1024,64]{1,2,0:T(8,128)(2,1)}, bf16[4,1024,64]{1,2,0:T(8,128)(2,1)}, bf16[4,1024,64]{1,2,...) while((s32[]{:T(128)}, f32[4,256,3,64]{1,3,2,0:T(8,128)}, ...), condition=%wide.region_26.27_spmd.clone, body=%wide.region_24.26_spmd.clone.sunk | while | flops 512228608 | bytes 26738976 | solution.py:278
  1052.6 15.7 copy.142
  1134.0 18.0 %reduce-scatter.39.cloned.1.call-done = bf16[384,2560]{1,0:T(8,128)(2,1)} async-done(((bf16[1536,2560]{1,0:T(8,128)(2,1)}), bf16[384,2560]{1,0:T(8,128)(2,1)}) %reduce-scatter.39.cloned.1.call-update) | async-done | bytes 1966096
  1166.7 56.9 %reduce-scatter.35.cloned.1.call-done = bf16[10,384,256]{2,1,0:T(8,128)(2,1)} async-done(((bf16[10,1536,256]{2,1,0:T(8,128)(2,1)}), bf16[10,384,256]{2,1,0:T(8,128)(2,1)}) %reduce-scatter.35.cloned.1.call-update) | async-done | bytes 1966096 | tf_op jit(solution)/shard_map/reduce_scatter | solution.py:336
  1227.4 67.9 %reduce-scatter.33.cloned.1.call-done = bf16[10,384,256]{2,1,0:T(8,128)(2,1)} async-done(((bf16[10,1536,256]{2,1,0:T(8,128)(2,1)}), bf16[10,384,256]{2,1,0:T(8,128)(2,1)}) %reduce-scatter.33.cloned.1.call-update) | async-done | bytes 1966096 | tf_op jit(solution)/shard_map/reduce_scatter | solution.py:333
  1300.1 55.3 %reduce-scatter.37.cloned.1.call-done = f32[96,40]{1,0:T(8,128)} async-done(((f32[1536,40]{1,0:T(8,128)}), f32[96,40]{1,0:T(8,128)}) %reduce-scatter.37.cloned.1.call-update) | async-done | bytes 15376
  1356.9 34.1 %all-reduce.8.cloned.1.call-done = bf16[256,1536]{1,0:T(8,128)(2,1)} async-done(((bf16[256,1536]{1,0:T(8,128)(2,1)}), bf16[256,1536]{1,0:T(8,128)(2,1)}) %all-reduce.8.cloned.1.call-update) | async-done | bytes 786448 | tf_op jit(solution)/shard_map/psum | solution.py:318
  1392.6 61.7 %all-reduce.2 = (f32[1536]{0:T(1024)S(1)}, f32[1536]{0:T(1024)S(1)}) all-reduce(f32[1536]{0:T(1024)S(1)} %get-tuple-element.172, f32[1536]{0:T(1024)S(1)} %copy-done.40), channel_id=6, replica_groups=mesh['dp'=4,'expert'=4,'tensor'=2] {'dp','expert'}, use_global_device_ids=true, to_apply=%region_32.33.clone | all-reduce | flops 3072 | bytes 24576
  1458.8 59.2 %reduce-scatter.29.cloned.1.call-done = f32[96,256]{1,0:T(8,128)} async-done(((f32[1536,256]{1,0:T(8,128)}), f32[96,256]{1,0:T(8,128)}) %reduce-scatter.29.cloned.1.call-update) | async-done | bytes 98320 | tf_op jit(solution)/shard_map/reduce_scatter | solution.py:326
  1518.0 79.1 %reduce-scatter.31.cloned.1.call-done = f32[768,96]{0,1:T(8,128)} async-done(((f32[768,1536]{0,1:T(8,128)}), f32[768,96]{0,1:T(8,128)}) %reduce-scatter.31.cloned.1.call-update) | async-done | bytes 294928 | tf_op jit(solution)/shard_map/reduce_scatter | solution.py:327
  1597.0 79.4 %reduce-scatter.25.cloned.1.call-done = f32[96,768]{1,0:T(8,128)} async-done(((f32[1536,768]{1,0:T(8,128)}), f32[96,768]{1,0:T(8,128)}) %reduce-scatter.25.cloned.1.call-update) | async-done | bytes 294928 | tf_op jit(solution)/shard_map/reduce_scatter | solution.py:324
  (309 shorter events, 368.5 us)
Async XLA Ops:
  7.2 77.8 %copy-start = (bf16[768,1536]{1,0:T(8,128)(2,1)S(1)}, bf16[768,1536]{1,0:T(8,128)(2,1)}, u32[]{:S(2)}) copy-start(bf16[768,1536]{1,0:T(8,128)(2,1)} %param.26) | copy-start | bytes 7077892
  7.2 115.0 %all-reduce.6.cloned.1.call-start = ((), (), s32[]{:S(2)}) async-start(), calls=%async_computation.16 | async-start | bytes 1572864 | tf_op jit(solution)/shard_map/psum | solution.py:124
  9.9 40.6 %copy-start.32 = (f32[256]{0:T(256)}, f32[256]{0:T(256)S(1)}, u32[]{:S(2)}) copy-start(f32[256]{0:T(256)S(1)} %get-tuple-element.239) | copy-start | bytes 3076
  13.2 40.1 %copy-start.17 = (f32[256,32]{0,1:T(8,128)}, f32[256,32]{0,1:T(8,128)S(1)}, u32[]{:S(2)}) copy-start(f32[256,32]{0,1:T(8,128)S(1)} %get-tuple-element.237) | copy-start | bytes 98308
  142.7 219.8 %all-to-all-start = ((bf16[40,80,1536]{2,1,0:T(8,128)(2,1)}), bf16[40,80,1536]{2,1,0:T(8,128)(2,1)}, u32[]{:S(2)}, u32[]{:S(2)}) async-start(bf16[40,80,1536]{2,1,0:T(8,128)(2,1)} %bitcast.354), calls=%async_computation | async-start | bytes 19660800 | tf_op jit(solution)/shard_map/all_to_all | solution.py:145
  362.5 219.3 %all-to-all-start.2 = ((bf16[40,80,1536]{2,1,0:T(8,128)(2,1)}), bf16[40,80,1536]{2,1,0:T(8,128)(2,1)}, u32[]{:S(2)}, u32[]{:S(2)}) async-start(bf16[40,80,1536]{2,1,0:T(8,128)(2,1)} %bitcast.355), calls=%async_computation.3 | async-start | bytes 19660800 | tf_op jit(solution)/shard_map/all_to_all | solution.py:198
  368.3 348.8 %reduce-scatter.17.cloned.1.call-start = ((), (), s32[]{:S(2)}) async-start(), calls=%async_computation.17 | async-start | bytes 14745600 | tf_op jit(solution)/shard_map/reduce_scatter | solution.py:152
  604.0 230.3 %reduce-scatter.19.cloned.1.call-start = ((), (), s32[]{:S(2)}) async-start(), calls=%async_computation.18 | async-start | bytes 14745600 | tf_op jit(solution)/shard_map/reduce_scatter | solution.py:227
  722.1 117.2 %all-to-all-start.1 = ((bf16[40,80,768]{2,1,0:T(8,128)(2,1)}), bf16[40,80,768]{2,1,0:T(8,128)(2,1)}, u32[]{:S(2)}, u32[]{:S(2)}) async-start(bf16[40,80,768]{2,1,0:T(8,128)(2,1)} %bitcast.358), calls=%async_computation.2 | async-start | bytes 9830400 | tf_op jit(solution)/shard_map/all_to_all | solution.py:160
  839.3 113.9 %all-to-all-start.3 = ((bf16[40,80,768]{2,1,0:T(8,128)(2,1)}), bf16[40,80,768]{2,1,0:T(8,128)(2,1)}, u32[]{:S(2)}, u32[]{:S(2)}) async-start(bf16[40,80,768]{2,1,0:T(8,128)(2,1)} %bitcast.357), calls=%async_computation.5 | async-start | bytes 9830400 | tf_op jit(solution)/shard_map/all_to_all | solution.py:230
  844.2 266.9 %reduce-scatter.21.cloned.1.call-start = ((), (), s32[]{:S(2)}) async-start(), calls=%async_computation.19 | async-start | bytes 655360 | tf_op jit(solution)/shard_map/reduce_scatter | solution.py:284
  878.8 111.6 %copy-start.31 = (bf16[256,40]{0,1:T(8,128)(2,1)}, bf16[256,40]{0,1:T(8,128)(2,1)S(1)}, u32[]{:S(2)}) copy-start(bf16[256,40]{0,1:T(8,128)(2,1)S(1)} %select_reduce_fusion) | copy-start | bytes 61444
  1040.1 76.0 %reduce-scatter.23.cloned.1.call-start = ((), (), s32[]{:S(2)}) async-start(), calls=%async_computation.20 | async-start | bytes 655360 | tf_op jit(solution)/shard_map/reduce_scatter | solution.py:287
  1040.7 111.3 %reduce-scatter.39.cloned.1.call-start = ((), (), s32[]{:S(2)}) async-start(), calls=%async_computation.29 | async-start | bytes 9830400
  1081.3 142.3 %reduce-scatter.35.cloned.1.call-start = ((), (), s32[]{:S(2)}) async-start(), calls=%async_computation.27 | async-start | bytes 9830400 | tf_op jit(solution)/shard_map/reduce_scatter | solution.py:336
  1091.1 204.2 %reduce-scatter.33.cloned.1.call-start = ((), (), s32[]{:S(2)}) async-start(), calls=%async_computation.26 | async-start | bytes 9830400 | tf_op jit(solution)/shard_map/reduce_scatter | solution.py:333
  1102.5 252.9 %reduce-scatter.37.cloned.1.call-start = ((), (), s32[]{:S(2)}) async-start(), calls=%async_computation.28 | async-start | bytes 835584
  1111.0 280.0 %all-reduce.8.cloned.1.call-start = ((), (), s32[]{:S(2)}) async-start(), calls=%async_computation.21 | async-start | bytes 1572864 | tf_op jit(solution)/shard_map/psum | solution.py:318
  1119.2 339.6 %reduce-scatter.27.cloned.1.call-start = ((), (), s32[]{:S(2)}) async-start(), calls=%async_computation.23 | async-start | bytes 1671168 | tf_op jit(solution)/shard_map/reduce_scatter | solution.py:325
  1120.9 397.0 %reduce-scatter.29.cloned.1.call-start = ((), (), s32[]{:S(2)}) async-start(), calls=%async_computation.24 | async-start | bytes 1671168 | tf_op jit(solution)/shard_map/reduce_scatter | solution.py:326
  1123.7 473.3 %reduce-scatter.31.cloned.1.call-start = ((), (), s32[]{:S(2)}) async-start(), calls=%async_computation.25 | async-start | bytes 5013504 | tf_op jit(solution)/shard_map/reduce_scatter | solution.py:327
  1128.1 548.3 %reduce-scatter.25.cloned.1.call-start = ((), (), s32[]{:S(2)}) async-start(), calls=%async_computation.22 | async-start | bytes 5013504 | tf_op jit(solution)/shard_map/reduce_scatter | solution.py:324
  1299.3 93.3 %copy-start.40 = (f32[1536]{0:T(1024)S(1)}, f32[1536]{0:T(1024)}, u32[]{:S(2)}) copy-start(f32[1536]{0:T(1024)} %get-tuple-element.170) | copy-start | bytes 18436
  1299.3 156.3 %copy-start.41 = (f32[256]{0:T(256)S(1)}, f32[256]{0:T(256)}, u32[]{:S(2)}) copy-start(f32[256]{0:T(256)} %get-tuple-element.238) | copy-start | bytes 3076
  (53 other events, 339.0 us)
Sparse Core Ops, SparseCore 0:
  86.8 34.7 all-reduce.5
  604.1 112.9 reduce-scatter.16
  719.4 114.7 reduce-scatter.18
  1040.2 19.6 reduce-scatter.20
  1062.1 19.9 reduce-scatter.22
  1084.7 67.2 reduce-scatter.38
  1154.5 68.9 reduce-scatter.34
  1226.3 68.9 reduce-scatter.32
  1298.9 56.5 reduce-scatter.36
  1357.7 33.3 all-reduce.7
  1395.3 59.6 reduce-scatter.26
  1459.5 58.4 reduce-scatter.28
  1522.4 74.5 reduce-scatter.30
  1601.8 74.5 reduce-scatter.24
where the time goes:
time: 1700 us; the launch traced here: 1680 us
  waiting for transfers between devices  1100 us (65%)
  matrix products  185 us (11%)
  local copies, waits for them, and re-layouts  122 us (7%)
  other arithmetic  122 us (7%)
  blocking collectives  113 us (7%)
  starting transfers between devices  23.2 us (1%)
    all_to_all x1, waiting for transfers between devices, body(): lax.all_to_all(dispatched, 'expert', split_axis=0, concat_axis=0, tiled=T...  194 us
    all_to_all x1, waiting for transfers between devices, body(): lax.all_to_all(cot_buffer, 'expert', split_axis=0, concat_axis=0, tiled=T...  192 us
    reduce_scatter x1, waiting for transfers between devices, body(): lax.psum_scatter(partial_in_grad.astype(jnp.bfloat16), 'tensor', scatter_...  107 us
    reduce_scatter x1, waiting for transfers between devices, body(): lax.psum_scatter(jnp.einsum('secf,efd->secd', activated, w_down, preferre...  84.1 us
    reduce_scatter x1, waiting for transfers between devices, body(): lax.psum_scatter(grad_query, ('dp', 'expert'), scatter_dimension=0, tiled...  79.4 us
    reduce_scatter x1, waiting for transfers between devices, body(): lax.psum_scatter(grad_out, ('dp', 'expert'), scatter_dimension=1, tiled=T...  79.1 us
    all_to_all x1, waiting for transfers between devices, body(): lax.all_to_all(in_grad_half.reshape(total_experts, capacity, half_width)....  74.3 us
    unnamed x16, waiting for transfers between devices  74 us
  transfers between devices with their start and end apart: 18, of which 13 were waited for; matrix products, arithmetic and copies ran while one was open for 16% of the time, Pallas kernels for 0%

commit v1 on v0

v1 whole, which is shorter than its diff:
```python
import jax
import jax.numpy as jnp
from jax import lax
from jax.sharding import PartitionSpec as P

HEAD_DIM = 64


EPSILON = 1e-05
ROPE_BASE = 10000.0
MASKED = -1e30


def rotate(values, positions, direction):
    head_size = values.shape[-1]
    half_dim = head_size // 2
    inverse = ROPE_BASE ** (-2.0 * jnp.arange(half_dim, dtype=jnp.float32) / head_size)
    angles = positions.astype(jnp.float32)[:, None] * inverse[None, :]
    cosine = jnp.cos(angles)[:, None, :]
    sine = direction * jnp.sin(angles)[:, None, :]
    first_half = values[..., :half_dim]
    second_half = values[..., half_dim:]
    return jnp.concatenate(
        [first_half * cosine - second_half * sine, second_half * cosine + first_half * sine],
        axis=-1,
    )


def norm_forward(values, gain):
    norm_scale = lax.rsqrt(jnp.mean(values * values, axis=1, keepdims=True) + EPSILON)
    return (norm_scale, values * norm_scale * gain)


def norm_backward(values, norm_scale, gain, grad_normed):
    weighted = grad_normed * gain
    inner = jnp.mean(weighted * values, axis=1, keepdims=True)
    grad_values = norm_scale * weighted - values * (norm_scale * norm_scale * norm_scale) * inner
    grad_gain = jnp.sum(grad_normed * values * norm_scale, axis=0)
    return (grad_values, grad_gain)


def swap(values, axis, bit=1):
    count = lax.axis_size(axis)
    return lax.ppermute(values, axis, [(i, i ^ bit) for i in range(count)])


def fetch(values, offset):
    count = lax.axis_size("expert")
    return lax.ppermute(values, "expert", [(i, (i - offset) % count) for i in range(count)])


def deliver(values, offset):
    count = lax.axis_size("expert")
    return lax.ppermute(values, "expert", [(i, (i + offset) % count) for i in range(count)])


def gather_blocks(rows, side):
    half = rows.shape[0] // 2
    own = lax.dynamic_slice_in_dim(rows, side * half, half)
    other = lax.dynamic_slice_in_dim(rows, (1 - side) * half, half)
    blocks = [(own, other)]
    for offset in range(1, lax.axis_size("expert")):
        far = fetch(own, offset)
        blocks.append((far, swap(far, "tensor")))
    return jnp.stack([jnp.concatenate(pair, axis=0) for pair in blocks])


def reduce_blocks(partial):
    blocks, rows, width = partial.shape
    half = rows // 2
    total = None
    for offset in range(blocks - 1, -1, -1):
        mine = partial[offset, :half].astype(jnp.float32)
        got = swap(partial[offset, half:], "tensor").astype(jnp.float32)
        piece = mine + got
        if offset:
            piece = deliver(piece.astype(jnp.bfloat16), offset).astype(jnp.float32)
        total = piece if total is None else total + piece
    return total


def halve(parts, bit_axis, bit):
    pairs = parts.reshape((parts.shape[0] // 2, 2) + parts.shape[1:])
    own = (lax.axis_index(bit_axis) // bit) % 2
    keep = lax.dynamic_index_in_dim(pairs, own, 1, keepdims=False)
    send = lax.dynamic_index_in_dim(pairs, 1 - own, 1, keepdims=False)
    got = swap(send, bit_axis, bit)
    return keep.astype(jnp.float32) + got.astype(jnp.float32)


def sum_over_dp(parts):
    bit = 1
    while parts.shape[0] > 1:
        parts = halve(parts.astype(jnp.bfloat16), "dp", bit)
        bit *= 2
    return parts[0]


def sum_over_tokens(rows):
    devices = lax.axis_size("dp") * lax.axis_size("expert")
    n_exp = lax.axis_size("expert")
    width = rows.shape[1]
    parts = rows.reshape(lax.axis_size("dp"), -1, width)
    bit = 1
    step = lax.axis_size("dp")
    parts = halve(parts, "dp", bit).astype(jnp.bfloat16)
    m = parts.shape[0]
    parts = parts.reshape(m, n_exp, -1, width)
    place = lax.axis_index("expert")
    total = lax.dynamic_index_in_dim(parts, place, 1, keepdims=False).astype(jnp.float32)
    for offset in range(1, n_exp):
        piece = lax.dynamic_index_in_dim(parts, (place + offset) % n_exp, 1, keepdims=False)
        total = total + deliver(piece, offset).astype(jnp.float32)
    bit = 2
    while total.shape[0] > 1:
        total = halve(total.astype(jnp.bfloat16), "dp", bit)
        bit *= 2
    return total[0]


def body(
    x_in,
    segments,
    chosen,
    out_grad,
    norm1_gain,
    w_query,
    w_key,
    w_value,
    w_out,
    norm2_gain,
    w_router,
    w_gate,
    w_up,
    w_down,
):
    tok_rows, full_width = x_in.shape
    head_size = HEAD_DIM
    kv_local = w_key.shape[1] // head_size
    query_local = w_query.shape[1] // head_size
    groups = query_local // kv_local
    experts_local = w_gate.shape[0]
    expert_devices = lax.axis_size("expert")
    tensor_devices = lax.axis_size("tensor")
    total_experts = experts_local * expert_devices
    top_count = chosen.shape[1]
    dp_devices = lax.axis_size("dp")
    capacity = tok_rows * top_count * 25 // (16 * total_experts)
    place = lax.axis_index("expert")
    side = lax.axis_index("tensor")
    half_width = full_width // tensor_devices
    row_start = lax.axis_index("expert") * tok_rows
    seq_length = segments.shape[0]
    positions = row_start + jnp.arange(tok_rows, dtype=jnp.int32)
    key_positions = jnp.arange(seq_length, dtype=jnp.int32)
    query_segments = lax.dynamic_slice_in_dim(segments, row_start, tok_rows)
    key_mask = (query_segments[:, None] == segments[None, :]) & (
        positions[:, None] >= key_positions[None, :]
    )
    score_scale = head_size ** (-0.5)
    inputs = x_in.astype(jnp.float32)
    scale_one, normed_one = norm_forward(inputs, norm1_gain)
    normed_one = normed_one.astype(jnp.bfloat16)
    query_pre = jnp.dot(normed_one, w_query, preferred_element_type=jnp.float32)
    key_pre = jnp.dot(normed_one, w_key, preferred_element_type=jnp.float32)
    value_pre = jnp.dot(normed_one, w_value, preferred_element_type=jnp.float32)
    query_rot = rotate(query_pre.reshape(tok_rows, query_local, head_size), positions, 1.0).astype(
        jnp.bfloat16
    )
    key_rot = (
        rotate(key_pre.reshape(tok_rows, kv_local, head_size), positions, 1.0)
        .astype(jnp.bfloat16)
        .reshape(tok_rows, kv_local * head_size)
    )
    value_low = value_pre.astype(jnp.bfloat16)
    kv_own = jnp.concatenate([key_rot, value_low], axis=1)
    kv_blocks = [kv_own] + [fetch(kv_own, k) for k in range(1, expert_devices)]
    kv_stack = jnp.stack(kv_blocks)
    kv_all = jnp.take(kv_stack, (jnp.arange(expert_devices) - place) % expert_devices, axis=0).reshape(seq_length, -1)
    keys_all, values_all = kv_all[:, : kv_local * head_size], kv_all[:, kv_local * head_size :]
    cot_in, chosen_in, kv_all = lax.optimization_barrier((out_grad, chosen, kv_all))
    cot_blocks = gather_blocks(cot_in, side)
    chosen_flip = jnp.where(side == 0, chosen_in, jnp.roll(chosen_in, tok_rows // 2, axis=0)).T
    chosen_blocks = jnp.stack([chosen_flip] + [fetch(chosen_flip, k) for k in range(1, expert_devices)])
    expert_ids = jnp.arange(total_experts, dtype=jnp.int32)
    hot_all = jnp.any(chosen_blocks[:, :, :, None] == expert_ids, axis=1)
    hot_local = lax.dynamic_slice_in_dim(hot_all, place * experts_local, experts_local, 2)
    token_row = jnp.arange(tok_rows, dtype=jnp.int32)
    before = (token_row[:, None] > token_row[None, :]).astype(jnp.bfloat16)
    rank = jnp.einsum("ts,kse->kte", before, hot_local.astype(jnp.bfloat16), preferred_element_type=jnp.float32).astype(jnp.int32)
    slot_of = jnp.where(hot_local, rank, -1).transpose(0, 2, 1)
    slot_hit = slot_of[:, :, None, :] == jnp.arange(capacity, dtype=jnp.int32)[:, None]
    pick = slot_hit.astype(jnp.bfloat16)
    pick_flat = pick.reshape(expert_devices, experts_local * capacity, tok_rows)
    cot_slots = jnp.einsum("kst,ktd->ksd", pick_flat, cot_blocks, preferred_element_type=jnp.float32).astype(jnp.bfloat16).reshape(expert_devices, experts_local, capacity, full_width)
    raw_grad = jnp.einsum("kesd,efd->kesf", cot_slots, w_down, preferred_element_type=jnp.float32)
    query_heads = query_rot.reshape(tok_rows, kv_local, groups, head_size).transpose(1, 0, 2, 3)
    key_heads = keys_all.reshape(seq_length, kv_local, head_size).transpose(1, 0, 2)
    value_heads = values_all.reshape(seq_length, kv_local, head_size).transpose(1, 0, 2)

    def head_forward(operands):
        q_head, k_head, v_head = operands
        scores = (
            jnp.einsum("qgd,kd->gqk", q_head, k_head, preferred_element_type=jnp.float32)
            * score_scale
        )
        scores = jnp.where(key_mask[None], scores, MASKED)
        row_peak = jnp.max(scores, axis=2, keepdims=True)
        raw_weights = jnp.exp(scores - row_peak)
        row_total = jnp.sum(raw_weights, axis=2, keepdims=True)
        probs_low = (raw_weights / row_total).astype(jnp.bfloat16)
        head_out = jnp.einsum("gqk,kd->qgd", probs_low, v_head, preferred_element_type=jnp.float32)
        return (head_out, (row_peak + jnp.log(row_total))[:, :, 0])

    attended_heads, log_totals = lax.map(head_forward, (query_heads, key_heads, value_heads))
    attended_low = (
        attended_heads.transpose(1, 0, 2, 3)
        .reshape(tok_rows, query_local * head_size)
        .astype(jnp.bfloat16)
    )
    head_partial = jnp.dot(attended_low, w_out, preferred_element_type=jnp.float32)
    head_low = head_partial.astype(jnp.bfloat16)
    hidden_one = inputs + head_low.astype(jnp.float32) + swap(head_low, "tensor").astype(jnp.float32)
    scale_two, normed_two = norm_forward(hidden_one, norm2_gain)
    normed_two = normed_two.astype(jnp.bfloat16)
    def gates_of(rows, hot):
        logits = jnp.dot(rows, w_router, preferred_element_type=jnp.float32)
        masked = jnp.where(hot, logits, MASKED)
        raw = jnp.where(hot, jnp.exp(masked - jnp.max(masked, axis=-1, keepdims=True)), 0.0)
        return raw / jnp.sum(raw, axis=-1, keepdims=True)

    token_blocks = gather_blocks(normed_two, side)
    gates_all = gates_of(token_blocks, hot_all)
    gates_local = lax.dynamic_slice_in_dim(gates_all, place * experts_local, experts_local, 2).transpose(0, 2, 1)
    gate_slots = jnp.sum(jnp.where(slot_hit, gates_local[:, :, None, :], 0.0), axis=3)[..., None]
    row_slots = jnp.einsum("kst,ktd->ksd", pick_flat, token_blocks, preferred_element_type=jnp.float32).astype(jnp.bfloat16).reshape(expert_devices, experts_local, capacity, full_width)
    gate_pre = jnp.einsum("kesd,edf->kesf", row_slots, w_gate, preferred_element_type=jnp.float32)
    up_pre = jnp.einsum("kesd,edf->kesf", row_slots, w_up, preferred_element_type=jnp.float32)
    sigmoid_gate = jax.nn.sigmoid(gate_pre)
    swish_gate = gate_pre * sigmoid_gate
    activated = swish_gate * up_pre
    dgate_slots = jnp.sum(activated * raw_grad, axis=3)
    gated = (gate_slots * activated).astype(jnp.bfloat16)
    activated_grad = gate_slots * raw_grad
    gate_pre_grad = (activated_grad * up_pre * sigmoid_gate * (1.0 + gate_pre * (1.0 - sigmoid_gate))).astype(jnp.bfloat16)
    up_pre_grad = (activated_grad * swish_gate).astype(jnp.bfloat16)
    in_grad = (
        jnp.einsum("kesf,edf->kesd", gate_pre_grad, w_gate, preferred_element_type=jnp.float32)
        + jnp.einsum("kesf,edf->kesd", up_pre_grad, w_up, preferred_element_type=jnp.float32)
    ).astype(jnp.bfloat16).reshape(expert_devices, experts_local * capacity, full_width)
    in_grad_part = jnp.einsum("kst,ksd->ktd", pick_flat, in_grad, preferred_element_type=jnp.float32).astype(jnp.bfloat16)
    dgate_part = jnp.sum(jnp.where(slot_hit, dgate_slots[..., None], 0.0), axis=2)
    dgate_own = dgate_part + jnp.roll(swap(dgate_part, "tensor"), tok_rows // 2, axis=2)
    dgate_stack = jnp.stack([dgate_own[0]] + [deliver(dgate_own[k], k) for k in range(1, expert_devices)])
    dgate_dense = jnp.take(dgate_stack, (place - jnp.arange(expert_devices)) % expert_devices, axis=0).reshape(total_experts, tok_rows)
    dgate_dense = jnp.where(side == 0, dgate_dense, jnp.roll(dgate_dense, tok_rows // 2, axis=1)).T
    hot_own = jnp.any(chosen[:, :, None] == expert_ids, axis=1)
    gates_own = gates_of(normed_two, hot_own)
    logit_grads = (gates_own * (dgate_dense - jnp.sum(gates_own * dgate_dense, axis=1, keepdims=True))).astype(jnp.bfloat16)
    half_sum = reduce_blocks(in_grad_part).astype(jnp.bfloat16)
    half_other = swap(half_sum, "tensor")
    expert_grad = jnp.where(
        side == 0,
        jnp.concatenate([half_sum, half_other], axis=0),
        jnp.concatenate([half_other, half_sum], axis=0),
    ).astype(jnp.float32)
    out_slots = jnp.einsum("kesf,efd->kesd", gated, w_down, preferred_element_type=jnp.float32).astype(jnp.bfloat16).reshape(expert_devices, experts_local * capacity, full_width)
    out_part = jnp.einsum("kst,ksd->ktd", pick_flat, out_slots, preferred_element_type=jnp.float32).astype(jnp.bfloat16)
    out_mine = lax.dynamic_slice_in_dim(out_part, side * half_width, half_width, 2)
    out_else = lax.dynamic_slice_in_dim(out_part, (1 - side) * half_width, half_width, 2)
    out_got = jnp.roll(swap(out_else, "tensor"), tok_rows // 2, axis=1)
    out_sum = out_mine.astype(jnp.float32) + out_got.astype(jnp.float32)
    out_low = out_sum.astype(jnp.bfloat16)
    mixture_half = out_sum[0]
    for k in range(1, expert_devices):
        mixture_half = mixture_half + deliver(out_low[k], k).astype(jnp.float32)
    mixture_half = jnp.where(side == 0, mixture_half, jnp.roll(mixture_half, tok_rows // 2, axis=0))
    residual_half = lax.dynamic_slice_in_dim(hidden_one, side * half_width, half_width, 1)
    block_out = (residual_half + mixture_half).astype(jnp.bfloat16)
    grad_down = jnp.einsum("kesf,kesd->efd", gated, cot_slots, preferred_element_type=jnp.float32).astype(jnp.bfloat16)
    grad_gate = jnp.einsum("kesd,kesf->edf", row_slots, gate_pre_grad, preferred_element_type=jnp.float32).astype(jnp.bfloat16)
    grad_up = jnp.einsum("kesd,kesf->edf", row_slots, up_pre_grad, preferred_element_type=jnp.float32).astype(jnp.bfloat16)
    inner = w_gate.shape[2]
    grad_gate = sum_over_dp(grad_gate.reshape(experts_local, dp_devices, -1, inner).transpose(1, 0, 2, 3))
    grad_up = sum_over_dp(grad_up.reshape(experts_local, dp_devices, -1, inner).transpose(1, 0, 2, 3))
    grad_down = sum_over_dp(grad_down.reshape(experts_local, inner, dp_devices, -1).transpose(2, 0, 1, 3))
    grad_router = jnp.einsum("rd,re->de", normed_two, logit_grads, preferred_element_type=jnp.float32)
    normed_two_grad = jnp.einsum("re,de->rd", logit_grads, w_router, preferred_element_type=jnp.float32)
    out_cot = out_grad.astype(jnp.float32)
    normed_two_grad = normed_two_grad + expert_grad
    hidden_grad, gain_two_grad = norm_backward(hidden_one, scale_two, norm2_gain, normed_two_grad)
    hidden_grad = hidden_grad + out_cot
    branch_cot = hidden_grad.astype(jnp.bfloat16)
    grad_out = jnp.einsum("rd,rh->dh", branch_cot, attended_low, preferred_element_type=jnp.float32)
    early = sum_over_tokens(
        jnp.concatenate([grad_out, grad_router, gain_two_grad[:, None]], axis=1).astype(jnp.bfloat16)
    )
    attended_grad = jnp.einsum(
        "rd,hd->rh", branch_cot, w_out, preferred_element_type=jnp.float32
    ).astype(jnp.bfloat16)
    grad_heads = attended_grad.reshape(tok_rows, kv_local, groups, head_size).transpose(1, 0, 2, 3)

    def head_backward(operands):
        q_head, k_head, v_head, d_head, o_head, lse_head = operands
        scores = (
            jnp.einsum("qgd,kd->gqk", q_head, k_head, preferred_element_type=jnp.float32)
            * score_scale
        )
        scores = jnp.where(key_mask[None], scores, MASKED)
        attention_probs = jnp.exp(scores - lse_head[:, :, None])
        probs_low = attention_probs.astype(jnp.bfloat16)
        value_part = jnp.einsum(
            "gqk,qgd->kd", probs_low, d_head, preferred_element_type=jnp.float32
        )
        probs_grad = jnp.einsum("qgd,kd->gqk", d_head, v_head, preferred_element_type=jnp.float32)
        delta_rows = jnp.sum(d_head.astype(jnp.float32) * o_head, axis=2).transpose(1, 0)
        scores_grad = (attention_probs * (probs_grad - delta_rows[:, :, None])).astype(jnp.bfloat16)
        query_part = (
            jnp.einsum("gqk,kd->qgd", scores_grad, k_head, preferred_element_type=jnp.float32)
            * score_scale
        )
        key_part = (
            jnp.einsum("gqk,qgd->kd", scores_grad, q_head, preferred_element_type=jnp.float32)
            * score_scale
        )
        return (query_part, key_part, value_part)

    query_grads, key_grads_all, value_grads_all = lax.map(
        head_backward, (query_heads, key_heads, value_heads, grad_heads, attended_heads, log_totals)
    )
    key_grad_rows = key_grads_all.transpose(1, 0, 2).reshape(seq_length, kv_local * head_size)
    value_grad_rows = value_grads_all.transpose(1, 0, 2).reshape(seq_length, kv_local * head_size)
    kv_grad = jnp.concatenate([key_grad_rows, value_grad_rows], axis=1).astype(jnp.bfloat16).reshape(expert_devices, tok_rows, -1)
    kv_sum = lax.dynamic_index_in_dim(kv_grad, place, 0, keepdims=False).astype(jnp.float32)
    for k in range(1, expert_devices):
        piece = lax.dynamic_index_in_dim(kv_grad, (place + k) % expert_devices, 0, keepdims=False)
        kv_sum = kv_sum + deliver(piece, k).astype(jnp.float32)
    key_grad_own, value_grad_own = kv_sum[:, : kv_local * head_size], kv_sum[:, kv_local * head_size :]
    query_grad = (
        rotate(
            query_grads.transpose(1, 0, 2, 3).reshape(tok_rows, query_local, head_size),
            positions,
            -1.0,
        )
        .astype(jnp.bfloat16)
        .reshape(tok_rows, query_local * head_size)
    )
    key_grad = (
        rotate(key_grad_own.reshape(tok_rows, kv_local, head_size), positions, -1.0)
        .astype(jnp.bfloat16)
        .reshape(tok_rows, kv_local * head_size)
    )
    value_grad = value_grad_own.astype(jnp.bfloat16)
    grad_query = jnp.einsum("rd,rh->dh", normed_one, query_grad, preferred_element_type=jnp.float32)
    grad_key = jnp.einsum("rd,rh->dh", normed_one, key_grad, preferred_element_type=jnp.float32)
    grad_value = jnp.einsum("rd,rh->dh", normed_one, value_grad, preferred_element_type=jnp.float32)
    normed_one_partial = jnp.einsum(
        "rh,dh->rd", query_grad, w_query, preferred_element_type=jnp.float32
    )
    normed_one_partial = normed_one_partial + jnp.einsum(
        "rh,dh->rd", key_grad, w_key, preferred_element_type=jnp.float32
    )
    normed_one_partial = normed_one_partial + jnp.einsum(
        "rh,dh->rd", value_grad, w_value, preferred_element_type=jnp.float32
    )
    partial_low = normed_one_partial.astype(jnp.bfloat16)
    normed_one_grad = partial_low.astype(jnp.float32) + swap(partial_low, "tensor").astype(jnp.float32)
    input_part, gain_one_grad = norm_backward(inputs, scale_one, norm1_gain, normed_one_grad)
    input_grad = hidden_grad + input_part
    late_query = sum_over_tokens(grad_query.astype(jnp.bfloat16))
    late = sum_over_tokens(
        jnp.concatenate([grad_key, grad_value, gain_one_grad[:, None]], axis=1).astype(jnp.bfloat16)
    )
    kv_width = kv_local * head_size
    q_width = query_local * head_size
    return (
        block_out,
        input_grad,
        late[:, 2 * kv_width],
        late_query,
        late[:, :kv_width],
        late[:, kv_width : 2 * kv_width],
        early[:, :q_width].T,
        early[:, q_width + total_experts],
        early[:, q_width : q_width + total_experts],
        grad_gate,
        grad_up,
        grad_down,
    )


def solution(mesh):
    return jax.shard_map(
        body,
        mesh=mesh,
        in_specs=(
            P(("dp", "expert"), None),
            P("dp"),
            P(("dp", "expert"), None),
            P(("dp", "expert"), None),
            P(),
            P(None, "tensor"),
            P(None, "tensor"),
            P(None, "tensor"),
            P("tensor", None),
            P(),
            P(),
            P("expert", None, "tensor"),
            P("expert", None, "tensor"),
            P("expert", "tensor", None),
        ),
        out_specs=(
            P(("dp", "expert"), "tensor"),
            P(("dp", "expert"), None),
            P(("dp", "expert")),
            P(("dp", "expert"), "tensor"),
            P(("dp", "expert"), "tensor"),
            P(("dp", "expert"), "tensor"),
            P("tensor", ("dp", "expert")),
            P(("dp", "expert")),
            P(("dp", "expert"), None),
            P("expert", "dp", "tensor"),
            P("expert", "dp", "tensor"),
            P("expert", "tensor", "dp"),
        ),
        check_vma=False,
    )
```

time: 1700 us -> 865 us (0.51)
  waiting for transfers between devices: 1100 us -> 323 us
  blocking collectives: 113 us -> 0 us
  starting transfers between devices: 23.2 us -> 86.4 us
  other arithmetic: 122 us -> 100 us
  local copies, waits for them, and re-layouts: 122 us -> 141 us
    reduce_scatter x10 -> x0, waiting for transfers between devices: 534 us -> none  [the longest x1 107 us: body(): lax.psum_scatter(partial_in_grad.astype(jnp.bfloat16), 'tensor', scatter_...]
    all_to_all x4 -> x0, waiting for transfers between devices: 460 us -> none  [the longest x1 194 us: body(): lax.all_to_all(dispatched, 'expert', split_axis=0, concat_axis=0, tiled=T...]
    ppermute x0 -> x60, waiting for transfers between devices: none -> 323 us  [the longest x27 183 us: swap(): return lax.ppermute(values, axis, [(i, i ^ bit) for i in range(count)])]
    ppermute x0 -> x60, starting transfers between devices: none -> 86.4 us  [the longest x21 48.4 us: deliver(): lax.ppermute(values, 'expert', [(i, (i + offset) % count) for i in range(...]
    unnamed x16 -> x0, waiting for transfers between devices: 74 us -> none
    unnamed x1 -> x0, blocking collectives: 61.7 us -> none
    all_gather x3 -> x0, blocking collectives: 46.5 us -> none  [the longest x1 18 us: body(): lax.all_gather(key_rot, 'expert', axis=0, tiled=True)]
    psum x2 -> x0, waiting for transfers between devices: 34.2 us -> none  [the longest x1 34.1 us: body(): lax.psum(normed_one_partial.astype(jnp.bfloat16), 'tensor')]
  transfers between devices with their start and end apart: 18 -> 60, of which waited for: 13 -> 27; matrix products, arithmetic and copies ran while one was open for 16% -> 34% of each run, Pallas kernels for 0% -> 0%
where the time goes in v1:
time: 865 us; the launch traced here: 854 us
  waiting for transfers between devices  323 us (37%)
  matrix products  201 us (23%)
  local copies, waits for them, and re-layouts  141 us (16%)
  other arithmetic  100 us (12%)
  starting transfers between devices  86.4 us (10%)
    ppermute x27, waiting for transfers between devices, swap(): return lax.ppermute(values, axis, [(i, i ^ bit) for i in range(count)])  183 us
    ppermute x21, waiting for transfers between devices, deliver(): lax.ppermute(values, 'expert', [(i, (i + offset) % count) for i in range(...  82 us
    ppermute x12, waiting for transfers between devices, fetch(): lax.ppermute(values, 'expert', [(i, (i - offset) % count) for i in range(...  57.8 us
    ppermute x21, starting transfers between devices, deliver(): lax.ppermute(values, 'expert', [(i, (i + offset) % count) for i in range(...  48.4 us
    squeeze x14, local copies, waits for them, and re-layouts, halve(): send = lax.dynamic_index_in_dim(pairs, 1 - own, 1, keepdims=False)  27.9 us
    ppermute x27, starting transfers between devices, swap(): return lax.ppermute(values, axis, [(i, i ^ bit) for i in range(count)])  21.6 us
  transfers between devices with their start and end apart: 60, of which 27 were waited for; matrix products, arithmetic and copies ran while one was open for 34% of the time, Pallas kernels for 0%

profile of v1, /device:TPU:0, one launch (start us, length us, event | category | flops | bytes accessed | tf_op | source)
XLA Modules:
  0.0 854.1 jit_solution(13780920564280028078)
XLA Ops:
  22.4 14.5 %collective-permute-done.1 = bf16[256,512]{0,1:T(8,128)(2,1)} collective-permute-done((bf16[256,512]{0,1:T(8,128)(2,1)}, bf16[256,512]{0,1:T(8,128)(2,1)}, u32[]{:S(2)}, u32[]{:S(2)}) %collective-permute-start.1) | collective-permute-done | bytes 262176 | tf_op jit(solution)/shard_map/ppermute | solution.py:49
  57.5 26.1 %while.28 = (s32[]{:T(128)}, f32[4,256,3,64]{1,3,2,0:T(8,128)}, f32[4,3,256]{2,1,0:T(4,128)}, bf16[4,1024,64]{1,2,0:T(8,128)(2,1)}, bf16[4,1024,64]{1,2,0:T(8,12...) while((s32[]{:T(128)}, f32[4,256,3,64]{1,3,2,0:T(8,128)}, ...), condition=%wide.region_4.5_spmd.clone, body=%wide.region_1.4_spmd.clone.sunk | while | flops 211549440 | bytes 11077221 | solution.py:215
  99.4 22.2 %collective-permute-done.19 = bf16[128,1536]{1,0:T(8,128)(2,1)S(1)} collective-permute-done((bf16[128,1536]{1,0:T(8,128)(2,1)S(1)}, bf16[128,1536]{1,0:T(8,128)(2,1)S(1)}, u32[]{:S(2)}, u32[]{:S(2)}) %collective-permute-start.19) | collective-permute-done | bytes 393248 | tf_op jit(solution)/shard_map/ppermute | solution.py:49
  145.6 13.9 %collective-permute-done.9 = bf16[128,1536]{1,0:T(8,128)(2,1)S(1)} collective-permute-done((bf16[128,1536]{1,0:T(8,128)(2,1)S(1)}, bf16[128,1536]{1,0:T(8,128)(2,1)S(1)}, u32[]{:S(2)}, u32[]{:S(2)}) %collective-permute-start.9) | collective-permute-done | bytes 393248 | tf_op jit(solution)/shard_map/ppermute | solution.py:49
  197.9 9.4 %fusion.73 = f32[10,4,80,256]{3,2,1,0:T(8,128)} fusion(bf16[4,10,80,1536]{3,2,1,0:T(8,128)(2,1)} %bitcast.610, bf16[10,1536,256]{2,1,0:T(8,128)(2,1)S(1)} %bitcast.563), kind=kOutput, calls=%fused_computation.87 | convolution fusion | flops 2516582400 | bytes 20971520 | tf_op jit(solution)/shard_map/kesd,edf->kesf/dot_general | solution.py:237
  207.2 12.1 %fusion.87 = (f32[4,10,80]{2,0,1:T(4,128)S(1)}, f32[10,4,80,256]{3,2,1,0:T(8,128)}) fusion(f32[10,4,80,256]{3,2,1,0:T(8,128)S(1)} %fusion.71, f32[10,4,80,256]{3,2,1,0:T(8,128)} %fusion.73, bf16[10,256,1536]{2,1,0:T(8,128)(2,1)} %param.31, bf16[4,10,80,1536]{3,2,1,0:T(8,128)(2,1)} %bitcast.607), kind=kOutput, calls=%fused_computation.120 | convolution fusion | flops 2522313728 | bytes 27537920 | tf_op jit(solution)/shard_map/kesd,efd->kesf/dot_general | solution.py:196
  227.6 9.9 %bitcast_convert_fusion.2 = bf16[10,1536,256]{2,1,0:T(8,128)(2,1)} fusion(bf16[4,10,80,1536]{3,2,1,0:T(8,128)(2,1)} %bitcast.611, bf16[4,10,80,256]{3,2,0,1:T(8,128)(2,1)S(1)} %get-tuple-element.303), kind=kOutput, calls=%fused_computation.75 | convolution fusion | flops 2520514560 | bytes 19333120 | tf_op jit(solution)/shard_map/kesd,kesf->edf/dot_general | solution.py:281
  237.5 12.6 %fusion.80 = f32[10,4,80,1536]{3,2,1,0:T(8,128)} fusion(bf16[4,10,80,256]{3,2,0,1:T(8,128)(2,1)S(1)} %get-tuple-element.303, bf16[10,1536,256]{2,1,0:T(8,128)(2,1)} %param.29), kind=kOutput, calls=%fused_computation.98 | convolution fusion | flops 2516582400 | bytes 29163520 | tf_op jit(solution)/shard_map/kesf,edf->kesd/dot_general | solution.py:248
  250.0 10.3 %bitcast_convert_fusion = bf16[10,256,1536]{2,1,0:T(8,128)(2,1)} fusion(bf16[4,10,80,256]{3,2,0,1:T(8,128)(2,1)S(1)} %get-tuple-element.304, bf16[4,10,80,1536]{3,2,1,0:T(8,128)(2,1)} %bitcast.608), kind=kOutput, calls=%fused_computation.73 | convolution fusion | flops 2520514560 | bytes 19333120 | tf_op jit(solution)/shard_map/kesf,kesd->efd/dot_general | solution.py:280
  260.3 8.4 fusion.66
  276.5 9.4 %bitcast_convert_fusion.1 = bf16[10,1536,256]{2,1,0:T(8,128)(2,1)} fusion(bf16[4,10,80,1536]{3,2,1,0:T(8,128)(2,1)} %bitcast.612, bf16[4,10,80,256]{3,2,0,1:T(8,128)(2,1)S(1)} %get-tuple-element.302), kind=kOutput, calls=%fused_computation.74 | convolution fusion | flops 2520514560 | bytes 19333120 | tf_op jit(solution)/shard_map/kesd,kesf->edf/dot_general | solution.py:282
  294.8 15.1 %fusion.65 = bf16[4,10,80,1536]{3,2,0,1:T(8,128)(2,1)} fusion(f32[10,4,80,1536]{3,2,1,0:T(8,128)} %fusion.80, bf16[4,10,80,256]{3,2,0,1:T(8,128)(2,1)} %copy-done.16, bf16[10,1536,256]{2,1,0:T(8,128)(2,1)} %param.30), kind=kOutput, calls=%fused_computation.79 | convolution fusion | flops 2526412800 | bytes 38993920 | tf_op jit(solution)/shard_map/kesf,edf->kesd/dot_general | solution.py:249
  309.8 8.5 copy.245
  328.7 8.5 copy.242
  397.4 9.8 %collective-permute-done.28 = bf16[128,1536]{1,0:T(8,128)(2,1)S(1)} collective-permute-done((bf16[128,1536]{1,0:T(8,128)(2,1)S(1)}, bf16[128,1536]{1,0:T(8,128)(2,1)S(1)}, u32[]{:S(2)}, u32[]{:S(2)}) %collective-permute-start.28) | collective-permute-done | bytes 393248 | tf_op jit(solution)/shard_map/ppermute | solution.py:54
  407.2 13.4 %collective-permute-done.30 = bf16[128,1536]{1,0:T(8,128)(2,1)S(1)} collective-permute-done((bf16[128,1536]{1,0:T(8,128)(2,1)S(1)}, bf16[128,1536]{1,0:T(8,128)(2,1)S(1)}, u32[]{:S(2)}, u32[]{:S(2)}) %collective-permute-start.30) | collective-permute-done | bytes 393248 | tf_op jit(solution)/shard_map/ppermute | solution.py:54
  423.9 14.2 %collective-permute-done.34 = bf16[128,1536]{1,0:T(8,128)(2,1)S(1)} collective-permute-done((bf16[128,1536]{1,0:T(8,128)(2,1)S(1)}, bf16[128,1536]{1,0:T(8,128)(2,1)S(1)}, u32[]{:S(2)}, u32[]{:S(2)}) %collective-permute-start.34) | collective-permute-done | bytes 393248 | tf_op jit(solution)/shard_map/ppermute | solution.py:44
  459.9 42.4 %while.29 = (s32[]{:T(128)}, f32[4,256,3,64]{1,3,2,0:T(8,128)}, bf16[4,1024,64]{1,2,0:T(8,128)(2,1)}, bf16[4,1024,64]{1,2,0:T(8,128)(2,1)}, bf16[4,1024,64]{1,2,...) while((s32[]{:T(128)}, f32[4,256,3,64]{1,3,2,0:T(8,128)}, ...), condition=%wide.region_19.20_spmd.clone, body=%wide.region_17.19_spmd.clone.sunk | while | flops 512228608 | bytes 22544608 | solution.py:328
  560.1 14.2 %collective-permute-done.15 = bf16[256,768]{1,0:T(8,128)(2,1)} collective-permute-done((bf16[256,768]{1,0:T(8,128)(2,1)}, bf16[256,768]{1,0:T(8,128)(2,1)}, u32[]{:S(2)}, u32[]{:S(2)}) %collective-permute-start.15) | collective-permute-done | bytes 393248 | tf_op jit(solution)/shard_map/ppermute | solution.py:54
  577.4 16.8 %collective-permute-done.38 = bf16[256,1536]{1,0:T(8,128)(2,1)S(1)} collective-permute-done((bf16[256,1536]{1,0:T(8,128)(2,1)S(1)}, bf16[256,1536]{1,0:T(8,128)(2,1)S(1)}, u32[]{:S(2)}, u32[]{:S(2)}) %collective-permute-start.38) | collective-permute-done | bytes 786464 | tf_op jit(solution)/shard_map/ppermute | solution.py:44
  623.6 9.7 %collective-permute-done.46 = bf16[2,96,768]{2,1,0:T(8,128)(2,1)} collective-permute-done((bf16[2,96,768]{2,1,0:T(8,128)(2,1)}, bf16[2,96,768]{2,1,0:T(8,128)(2,1)}, u32[]{:S(2)}, u32[]{:S(2)}) %collective-permute-start.46) | collective-permute-done | bytes 294944 | tf_op jit(solution)/shard_map/ppermute | solution.py:54
  654.4 17.2 %collective-permute-done.51 = bf16[2,96,809]{1,2,0:T(8,128)(2,1)S(1)} collective-permute-done((bf16[2,96,809]{1,2,0:T(8,128)(2,1)}, bf16[2,96,809]{1,2,0:T(8,128)(2,1)S(1)}, u32[]{:S(2)}, u32[]{:S(2)}) %collective-permute-start.51) | collective-permute-done | bytes 310688 | tf_op jit(solution)/shard_map/ppermute | solution.py:54
  687.6 9.0 %collective-permute-start.40 = (bf16[2,96,513]{2,1,0:T(8,128)(2,1)S(1)}, bf16[2,96,513]{2,1,0:T(8,128)(2,1)S(1)}, u32[]{:S(2)}, u32[]{:S(2)}) collective-permute-start(bf16[2,96,513]{2,1,0:T(8,128)(2,1)S(1)} %get-tuple-element.330), channel_id=1, source_target_pairs={{0,2},{2,4},{4,6},{6,0},{1,3},{3,5},{5,7},{7,1},{8,10},{10,12},{12... | collective-permute-start | bytes 590984 | tf_op jit(solution)/shard_map/ppermute | solution.py:54
  730.1 108.7 %collective-permute-done.43 = bf16[1,96,513]{2,1,0:T(8,128)(2,1)S(1)} collective-permute-done((bf16[1,96,513]{2,1,0:T(8,128)(2,1)S(1)}, bf16[1,96,513]{2,1,0:T(8,128)(2,1)S(1)}, u32[]{:S(2)}, u32[]{:S(2)}) %collective-permute-start.43) | collective-permute-done | bytes 98528 | tf_op jit(solution)/shard_map/ppermute | solution.py:44
  (519 shorter events, 483.9 us)
Async XLA Ops:
  47.5 41.8 %collective-permute-start.4 = (s32[8,256]{1,0:T(8,128)}, s32[8,256]{1,0:T(8,128)}, u32[]{:S(2)}, u32[]{:S(2)}) collective-permute-start(s32[8,256]{1,0:T(8,128)} %get-tuple-element.362), channel_id=1, source_target_pairs={{0,6},{2,0},{4,2},{6,4},{1,7},{3,1},{5,3},{7,5},{8,14},{10,8},{12,... | collective-permute-start | bytes 24584 | tf_op jit(solution)/shard_map/ppermute | solution.py:49
  47.5 41.8 %collective-permute-start.5 = (s32[8,256]{1,0:T(8,128)}, s32[8,256]{1,0:T(8,128)}, u32[]{:S(2)}, u32[]{:S(2)}) collective-permute-start(s32[8,256]{1,0:T(8,128)} %get-tuple-element.362), channel_id=1, source_target_pairs={{0,4},{2,6},{4,0},{6,2},{1,5},{3,7},{5,1},{7,3},{8,12},{10,14},{12... | collective-permute-start | bytes 24584 | tf_op jit(solution)/shard_map/ppermute | solution.py:49
  50.3 39.7 %collective-permute-start.6 = (s32[8,256]{1,0:T(8,128)}, s32[8,256]{1,0:T(8,128)}, u32[]{:S(2)}, u32[]{:S(2)}) collective-permute-start(s32[8,256]{1,0:T(8,128)} %get-tuple-element.362), channel_id=1, source_target_pairs={{0,2},{2,4},{4,6},{6,0},{1,3},{3,5},{5,7},{7,1},{8,10},{10,12},{12... | collective-permute-start | bytes 24584 | tf_op jit(solution)/shard_map/ppermute | solution.py:49
  85.7 37.9 %collective-permute-start.3 = (bf16[256,1536]{1,0:T(8,128)(2,1)S(1)}, bf16[256,1536]{1,0:T(8,128)(2,1)S(1)}, u32[]{:S(2)}, u32[]{:S(2)}) collective-permute-start(bf16[256,1536]{1,0:T(8,128)(2,1)S(1)} %convolution_convert_fusion.7), channel_id=1, source_target_pairs={{0,1},{1,0},{2,3},{3,2},{4,5},{5,4},{6,7},{7,6},{8,9},{9,8},{10,11... | collective-permute-start | bytes 2359304 | tf_op jit(solution)/shard_map/ppermute | solution.py:44
  89.2 32.3 %collective-permute-start.19 = (bf16[128,1536]{1,0:T(8,128)(2,1)S(1)}, bf16[128,1536]{1,0:T(8,128)(2,1)S(1)}, u32[]{:S(2)}, u32[]{:S(2)}) collective-permute-start(bf16[128,1536]{1,0:T(8,128)(2,1)S(1)} %get-tuple-element.344), channel_id=1, source_target_pairs={{0,4},{2,6},{4,0},{6,2},{1,5},{3,7},{5,1},{7,3},{8,12},{10,14},{12... | collective-permute-start | bytes 1179656 | tf_op jit(solution)/shard_map/ppermute | solution.py:49
  89.2 32.8 %collective-permute-start.21 = (bf16[128,1536]{1,0:T(8,128)(2,1)S(1)}, bf16[128,1536]{1,0:T(8,128)(2,1)S(1)}, u32[]{:S(2)}, u32[]{:S(2)}) collective-permute-start(bf16[128,1536]{1,0:T(8,128)(2,1)S(1)} %get-tuple-element.344), channel_id=1, source_target_pairs={{0,2},{2,4},{4,6},{6,0},{1,3},{3,5},{5,7},{7,1},{8,10},{10,12},{12... | collective-permute-start | bytes 1179656 | tf_op jit(solution)/shard_map/ppermute | solution.py:49
  98.9 27.3 %collective-permute-start.18 = (bf16[128,1536]{1,0:T(8,128)(2,1)S(1)}, bf16[128,1536]{1,0:T(8,128)(2,1)S(1)}, u32[]{:S(2)}, u32[]{:S(2)}) collective-permute-start(bf16[128,1536]{1,0:T(8,128)(2,1)S(1)} %collective-permute-done.17), channel_id=1, source_target_pairs={{0,1},{1,0},{2,3},{3,2},{4,5},{5,4},{6,7},{7,6},{8,9},{9,8},{10,11... | collective-permute-start | bytes 1179656 | tf_op jit(solution)/shard_map/ppermute | solution.py:44
  125.1 34.4 %collective-permute-start.9 = (bf16[128,1536]{1,0:T(8,128)(2,1)S(1)}, bf16[128,1536]{1,0:T(8,128)(2,1)S(1)}, u32[]{:S(2)}, u32[]{:S(2)}) collective-permute-start(bf16[128,1536]{1,0:T(8,128)(2,1)S(1)} %get-tuple-element.342), channel_id=1, source_target_pairs={{0,4},{2,6},{4,0},{6,2},{1,5},{3,7},{5,1},{7,3},{8,12},{10,14},{12... | collective-permute-start | bytes 1179656 | tf_op jit(solution)/shard_map/ppermute | solution.py:49
  126.1 35.9 %collective-permute-start.11 = (bf16[128,1536]{1,0:T(8,128)(2,1)S(1)}, bf16[128,1536]{1,0:T(8,128)(2,1)S(1)}, u32[]{:S(2)}, u32[]{:S(2)}) collective-permute-start(bf16[128,1536]{1,0:T(8,128)(2,1)S(1)} %get-tuple-element.342), channel_id=1, source_target_pairs={{0,2},{2,4},{4,6},{6,0},{1,3},{3,5},{5,7},{7,1},{8,10},{10,12},{12... | collective-permute-start | bytes 1179656 | tf_op jit(solution)/shard_map/ppermute | solution.py:49
  293.2 71.7 %collective-permute-start.23 = (f32[4,10,256]{2,1,0:T(8,128)S(1)}, f32[4,10,256]{2,1,0:T(8,128)S(1)}, u32[]{:S(2)}, u32[]{:S(2)}) collective-permute-start(f32[4,10,256]{2,1,0:T(8,128)S(1)} %get-tuple-element.248), channel_id=1, source_target_pairs={{0,1},{1,0},{2,3},{3,2},{4,5},{5,4},{6,7},{7,6},{8,9},{9,8},{10,11... | collective-permute-start | bytes 122888 | tf_op jit(solution)/shard_map/ppermute | solution.py:44
  364.4 27.2 %collective-permute-start.31 = (bf16[128,1536]{1,0:T(8,128)(2,1)S(1)}, bf16[128,1536]{1,0:T(8,128)(2,1)}, u32[]{:S(2)}, u32[]{:S(2)}) collective-permute-start(bf16[128,1536]{1,0:T(8,128)(2,1)S(1)} %copy-done.51), channel_id=1, source_target_pairs={{0,1},{1,0},{2,3},{3,2},{4,5},{5,4},{6,7},{7,6},{8,9},{9,8},{10,11... | collective-permute-start | bytes 1179656 | tf_op jit(solution)/shard_map/ppermute | solution.py:44
  375.0 325.2 %collective-permute-start.58 = (bf16[2,10,256,384]{3,2,1,0:T(8,128)(2,1)}, bf16[2,10,256,384]{3,2,1,0:T(8,128)(2,1)}, u32[]{:S(2)}, u32[]{:S(2)}) collective-permute-start(bf16[2,10,256,384]{3,2,1,0:T(8,128)(2,1)} %dynamic-slice_bitcast_fusion.1), channel_id=1, source_target_pairs={{0,8},{8,0},{16,24},{24,16},{1,9},{9,1},{17,25},{25,17},{2,10},{10... | collective-permute-start | bytes 11796488 | tf_op jit(solution)/shard_map/ppermute | solution.py:44
  393.5 27.1 %collective-permute-start.30 = (bf16[128,1536]{1,0:T(8,128)(2,1)S(1)}, bf16[128,1536]{1,0:T(8,128)(2,1)S(1)}, u32[]{:S(2)}, u32[]{:S(2)}) collective-permute-start(bf16[128,1536]{1,0:T(8,128)(2,1)S(1)} %get-tuple-element.307), channel_id=1, source_target_pairs={{0,4},{2,6},{4,0},{6,2},{1,5},{3,7},{5,1},{7,3},{8,12},{10,14},{12... | collective-permute-start | bytes 1179656 | tf_op jit(solution)/shard_map/ppermute | solution.py:54
  393.6 27.0 %collective-permute-start.32 = (bf16[128,1536]{1,0:T(8,128)(2,1)S(1)}, bf16[128,1536]{1,0:T(8,128)(2,1)S(1)}, u32[]{:S(2)}, u32[]{:S(2)}) collective-permute-start(bf16[128,1536]{1,0:T(8,128)(2,1)S(1)} %get-tuple-element.306), channel_id=1, source_target_pairs={{0,2},{2,4},{4,6},{6,0},{1,3},{3,5},{5,7},{7,1},{8,10},{10,12},{12... | collective-permute-start | bytes 1179656 | tf_op jit(solution)/shard_map/ppermute | solution.py:54
  396.9 141.5 %collective-permute-start.13 = (bf16[4,256,768]{2,1,0:T(8,128)(2,1)}, bf16[4,256,768]{2,1,0:T(8,128)(2,1)}, u32[]{:S(2)}, u32[]{:S(2)}) collective-permute-start(bf16[4,256,768]{2,1,0:T(8,128)(2,1)} %constant_dynamic-slice_fusion.15), channel_id=1, source_target_pairs={{0,1},{1,0},{2,3},{3,2},{4,5},{5,4},{6,7},{7,6},{8,9},{9,8},{10,11... | collective-permute-start | bytes 4718600 | tf_op jit(solution)/shard_map/ppermute | solution.py:44
  530.9 177.8 %collective-permute-start.56 = (bf16[2,10,384,256]{3,2,1,0:T(8,128)(2,1)}, bf16[2,10,384,256]{3,2,1,0:T(8,128)(2,1)}, u32[]{:S(2)}, u32[]{:S(2)}) collective-permute-start(bf16[2,10,384,256]{3,2,1,0:T(8,128)(2,1)} %dynamic-slice_bitcast_fusion.2), channel_id=1, source_target_pairs={{0,8},{8,0},{16,24},{24,16},{1,9},{9,1},{17,25},{25,17},{2,10},{10... | collective-permute-start | bytes 11796488 | tf_op jit(solution)/shard_map/ppermute | solution.py:44
  560.1 156.2 %collective-permute-start.54 = (bf16[2,10,384,256]{3,2,1,0:T(8,128)(2,1)}, bf16[2,10,384,256]{3,2,1,0:T(8,128)(2,1)}, u32[]{:S(2)}, u32[]{:S(2)}) collective-permute-start(bf16[2,10,384,256]{3,2,1,0:T(8,128)(2,1)} %dynamic-slice_bitcast_fusion.3), channel_id=1, source_target_pairs={{0,8},{8,0},{16,24},{24,16},{1,9},{9,1},{17,25},{25,17},{2,10},{10... | collective-permute-start | bytes 11796488 | tf_op jit(solution)/shard_map/ppermute | solution.py:44
  623.2 26.5 %collective-permute-start.47 = (bf16[2,96,768]{2,1,0:T(8,128)(2,1)}, bf16[2,96,768]{2,1,0:T(8,128)(2,1)}, u32[]{:S(2)}, u32[]{:S(2)}) collective-permute-start(bf16[2,96,768]{2,1,0:T(8,128)(2,1)} %get-tuple-element.322), channel_id=1, source_target_pairs={{0,6},{2,0},{4,2},{6,4},{1,7},{3,1},{5,3},{7,5},{8,14},{10,8},{12,... | collective-permute-start | bytes 884744 | tf_op jit(solution)/shard_map/ppermute | solution.py:54
  687.6 35.8 %collective-permute-start.40 = (bf16[2,96,513]{2,1,0:T(8,128)(2,1)S(1)}, bf16[2,96,513]{2,1,0:T(8,128)(2,1)S(1)}, u32[]{:S(2)}, u32[]{:S(2)}) collective-permute-start(bf16[2,96,513]{2,1,0:T(8,128)(2,1)S(1)} %get-tuple-element.330), channel_id=1, source_target_pairs={{0,2},{2,4},{4,6},{6,0},{1,3},{3,5},{5,7},{7,1},{8,10},{10,12},{12... | collective-permute-start | bytes 590984 | tf_op jit(solution)/shard_map/ppermute | solution.py:54
  696.6 28.5 %collective-permute-start.41 = (bf16[2,96,513]{2,1,0:T(8,128)(2,1)S(1)}, bf16[2,96,513]{2,1,0:T(8,128)(2,1)S(1)}, u32[]{:S(2)}, u32[]{:S(2)}) collective-permute-start(bf16[2,96,513]{2,1,0:T(8,128)(2,1)S(1)} %get-tuple-element.332), channel_id=1, source_target_pairs={{0,4},{2,6},{4,0},{6,2},{1,5},{3,7},{5,1},{7,3},{8,12},{10,14},{12... | collective-permute-start | bytes 590984 | tf_op jit(solution)/shard_map/ppermute | solution.py:54
  708.6 132.4 %collective-permute-start.59 = (bf16[1,10,256,384]{3,2,1,0:T(8,128)(2,1)}, bf16[1,10,256,384]{3,2,1,0:T(8,128)(2,1)}, u32[]{:S(2)}, u32[]{:S(2)}) collective-permute-start(bf16[1,10,256,384]{3,2,1,0:T(8,128)(2,1)} %constant_dynamic-slice_fusion), channel_id=1, source_target_pairs={{0,16},{8,24},{16,0},{24,8},{1,17},{9,25},{17,1},{25,9},{2,18},{10... | collective-permute-start | bytes 5898248 | tf_op jit(solution)/shard_map/ppermute | solution.py:44
  716.3 129.4 %collective-permute-start.57 = (bf16[1,10,384,256]{3,2,1,0:T(8,128)(2,1)}, bf16[1,10,384,256]{3,2,1,0:T(8,128)(2,1)}, u32[]{:S(2)}, u32[]{:S(2)}) collective-permute-start(bf16[1,10,384,256]{3,2,1,0:T(8,128)(2,1)} %constant_dynamic-slice_fusion.1), channel_id=1, source_target_pairs={{0,16},{8,24},{16,0},{24,8},{1,17},{9,25},{17,1},{25,9},{2,18},{10... | collective-permute-start | bytes 5898248 | tf_op jit(solution)/shard_map/ppermute | solution.py:44
  723.4 126.5 %collective-permute-start.55 = (bf16[1,10,384,256]{3,2,1,0:T(8,128)(2,1)}, bf16[1,10,384,256]{3,2,1,0:T(8,128)(2,1)}, u32[]{:S(2)}, u32[]{:S(2)}) collective-permute-start(bf16[1,10,384,256]{3,2,1,0:T(8,128)(2,1)} %constant_dynamic-slice_fusion.2), channel_id=1, source_target_pairs={{0,16},{8,24},{16,0},{24,8},{1,17},{9,25},{17,1},{25,9},{2,18},{10... | collective-permute-start | bytes 5898248 | tf_op jit(solution)/shard_map/ppermute | solution.py:44
  725.9 112.8 %collective-permute-start.43 = (bf16[1,96,513]{2,1,0:T(8,128)(2,1)S(1)}, bf16[1,96,513]{2,1,0:T(8,128)(2,1)S(1)}, u32[]{:S(2)}, u32[]{:S(2)}) collective-permute-start(bf16[1,96,513]{2,1,0:T(8,128)(2,1)S(1)} %constant_dynamic-slice_fusion.9), channel_id=1, source_target_pairs={{0,16},{8,24},{16,0},{24,8},{1,17},{9,25},{17,1},{25,9},{2,18},{10... | collective-permute-start | bytes 295496 | tf_op jit(solution)/shard_map/ppermute | solution.py:44
  (126 other events, 2020.9 us)

commit v2 on v1

v2 whole, which is shorter than its diff:
```python
import functools

import jax
import jax.numpy as jnp
import numpy as np
from jax import lax
from jax.experimental import pallas as pl
from jax.experimental.pallas import tpu as pltpu
from jax.sharding import PartitionSpec as P

HEAD_DIM = 64
EPSILON = 1e-05
ROPE_BASE = 10000.0
MASKED = -1e30
BF = jnp.bfloat16
F32 = jnp.float32
MIB = 1024 * 1024


def swap(values, axis, bit=1):
    count = lax.axis_size(axis)
    return lax.ppermute(values, axis, [(i, i ^ bit) for i in range(count)])


def fetch(values, offset):
    count = lax.axis_size("expert")
    return lax.ppermute(values, "expert", [(i, (i - offset) % count) for i in range(count)])


def deliver(values, offset):
    count = lax.axis_size("expert")
    return lax.ppermute(values, "expert", [(i, (i + offset) % count) for i in range(count)])


def gather_blocks(rows, side):
    half = rows.shape[0] // 2
    own = lax.dynamic_slice_in_dim(rows, side * half, half)
    other = lax.dynamic_slice_in_dim(rows, (1 - side) * half, half)
    blocks = [(own, other)]
    for offset in range(1, lax.axis_size("expert")):
        far = fetch(own, offset)
        blocks.append((far, swap(far, "tensor")))
    return jnp.stack([jnp.concatenate(pair, axis=0) for pair in blocks])


def reduce_blocks(partial):
    blocks, rows, width = partial.shape
    half = rows // 2
    total = None
    for offset in range(blocks - 1, -1, -1):
        mine = partial[offset, :half].astype(F32)
        got = swap(partial[offset, half:], "tensor").astype(F32)
        piece = mine + got
        if offset:
            piece = deliver(piece.astype(BF), offset).astype(F32)
        total = piece if total is None else total + piece
    return total


def halve(parts, bit_axis, bit):
    pairs = parts.reshape((parts.shape[0] // 2, 2) + parts.shape[1:])
    own = (lax.axis_index(bit_axis) // bit) % 2
    keep = lax.dynamic_index_in_dim(pairs, own, 1, keepdims=False)
    send = lax.dynamic_index_in_dim(pairs, 1 - own, 1, keepdims=False)
    got = swap(send, bit_axis, bit)
    return keep.astype(F32) + got.astype(F32)


def sum_over_dp(parts):
    bit = 1
    while parts.shape[0] > 1:
        parts = halve(parts.astype(BF), "dp", bit)
        bit *= 2
    return parts[0]


def sum_places(keep, send):
    bit = 1
    total = keep.astype(F32) + swap(send, "dp", bit).astype(F32)
    while total.shape[0] > 1:
        bit *= 2
        pairs = total.reshape((total.shape[0] // 2, 2) + total.shape[1:])
        total = pairs[:, 0] + swap(pairs[:, 1].astype(BF), "dp", bit).astype(F32)
    return total[0]


def sum_over_tokens(rows):
    n_exp = lax.axis_size("expert")
    width = rows.shape[1]
    parts = rows.reshape(lax.axis_size("dp"), -1, width)
    parts = halve(parts, "dp", 1).astype(BF)
    parts = parts.reshape(parts.shape[0], n_exp, -1, width)
    place = lax.axis_index("expert")
    total = lax.dynamic_index_in_dim(parts, place, 1, keepdims=False).astype(F32)
    for offset in range(1, n_exp):
        piece = lax.dynamic_index_in_dim(parts, (place + offset) % n_exp, 1, keepdims=False)
        total = total + deliver(piece, offset).astype(F32)
    bit = 2
    while total.shape[0] > 1:
        total = halve(total.astype(BF), "dp", bit)
        bit *= 2
    return total[0]


def nn(left, right):
    return jnp.dot(left, right, preferred_element_type=F32)


def nt(left, right):
    return lax.dot_general(left, right, (((1,), (1,)), ((), ())), preferred_element_type=F32)


def tn(left, right):
    return lax.dot_general(left, right, (((0,), (0,)), ((), ())), preferred_element_type=F32)


def params(mib):
    return pltpu.CompilerParams(vmem_limit_bytes=mib * MIB)


def full(shape):
    return pl.BlockSpec(shape, lambda *_: (0,) * len(shape))


def turned(values, cosine, sine):
    lane = lax.broadcasted_iota(jnp.int32, values.shape, 1)
    quarter = HEAD_DIM // 2
    later = pltpu.roll(values, 2 * HEAD_DIM - quarter, 1)
    earlier = pltpu.roll(values, quarter, 1)
    return values * cosine + jnp.where(lane % HEAD_DIM < quarter, later, earlier) * sine


def project_kernel(x_ref, gain_ref, wq_ref, wk_ref, wv_ref, cos_ref, sin_ref, n_ref, q_ref, kv_ref, s_ref):
    values = x_ref[...].astype(F32)
    scale = lax.rsqrt(jnp.mean(values * values, axis=1, keepdims=True) + EPSILON)
    s_ref[...] = scale
    normed = (values * scale * gain_ref[...]).astype(BF)
    n_ref[...] = normed
    cosine, sine = cos_ref[...], sin_ref[...]
    lanes = 2 * HEAD_DIM
    kv = wk_ref.shape[1]
    keys = nn(normed, wk_ref[...])
    for i in range(0, kv, lanes):
        kv_ref[:, i : i + lanes] = turned(keys[:, i : i + lanes], cosine, sine).astype(BF)
    kv_ref[:, kv:] = nn(normed, wv_ref[...]).astype(BF)
    query = nn(normed, wq_ref[...])
    for i in range(0, query.shape[1], lanes):
        q_ref[:, i : i + lanes] = turned(query[:, i : i + lanes], cosine, sine).astype(BF)


def attend_kernel(groups, q_ref, k_ref, v_ref, bias_ref, o_ref, lse_ref):
    h = HEAD_DIM
    rows = q_ref.shape[0]
    for kv in range(k_ref.shape[1] // h):
        key = k_ref[:, kv * h : kv * h + h]
        value = v_ref[:, kv * h : kv * h + h]
        for g in range(groups):
            head = kv * groups + g
            query = q_ref[:, head * h : head * h + h]
            scores = nt(query, key) * h**-0.5 + bias_ref[...]
            peak = jnp.max(scores, axis=1, keepdims=True)
            raw = jnp.exp(scores - peak)
            total = jnp.sum(raw, axis=1, keepdims=True)
            probs = (raw * (1.0 / total)).astype(BF)
            o_ref[:, head * h : head * h + h] = nn(probs, value)
            lse_ref[0, :, head : head + 1] = peak + jnp.log(total)


def attend_grad_kernel(groups, q_ref, k_ref, v_ref, d_ref, o_ref, lse_ref, bias_ref, dq_ref, dk_ref, dv_ref):
    h = HEAD_DIM
    for kv in range(k_ref.shape[1] // h):
        key = k_ref[:, kv * h : kv * h + h]
        value = v_ref[:, kv * h : kv * h + h]
        key_grad = value_grad = None
        for g in range(groups):
            head = kv * groups + g
            span = slice(head * h, head * h + h)
            query = q_ref[:, span]
            cot = d_ref[:, span]
            scores = nt(query, key) * h**-0.5 + bias_ref[...]
            probs = jnp.exp(scores - lse_ref[0, :, head : head + 1])
            delta = jnp.sum(cot.astype(F32) * o_ref[:, span], axis=1, keepdims=True)
            slope = (probs * (nt(cot, value) - delta)).astype(BF)
            value_part = tn(cot, probs.astype(BF))
            key_part = tn(query, slope)
            dq_ref[:, span] = nn(slope, key) * h**-0.5
            value_grad = value_part if value_grad is None else value_grad + value_part
            key_grad = key_part if key_grad is None else key_grad + key_part
        dk_ref[kv * h : kv * h + h, :] = (key_grad * h**-0.5).astype(BF)
        dv_ref[kv * h : kv * h + h, :] = value_grad.astype(BF)


def cotangent_kernel(pick_ref, cot_ref, wd_ref, cg_ref, dm_ref):
    blocks, _, slots, _ = pick_ref.shape
    for k in range(blocks):
        cg_ref[0, k * slots : (k + 1) * slots, :] = nn(pick_ref[k, 0], cot_ref[k]).astype(BF)
    dm_ref[0] = nt(cg_ref[0], wd_ref[0])


def experts_kernel(
    place_ref, x_ref, hot_ref, router_ref, pick_ref, spread_ref, dm_ref, wg_ref, wu_ref,
    xg_ref, gm_ref, da_ref, db_ref, dg_ref, dn_ref, gates_ref, n_ref,
):
    blocks, _, slots, rows = pick_ref.shape
    step, steps = pl.program_id(0), pl.num_programs(0)

    @pl.when(step == 0)
    def _():
        tokens = x_ref[...].reshape(blocks * rows, x_ref.shape[2])
        hot = hot_ref[...] > 0.0
        logits = jnp.where(hot, nt(router_ref[...], tokens), MASKED)
        raw = jnp.where(hot, jnp.exp(logits - jnp.max(logits, axis=0, keepdims=True)), 0.0)
        gates_ref[...] = raw / jnp.sum(raw, axis=0, keepdims=True)

    gate_row = gates_ref[pl.ds(place_ref[0] * steps + step, 1), :]
    gate_parts = []
    for k in range(blocks):
        pick = pick_ref[k, 0]
        xg_ref[0, k * slots : (k + 1) * slots, :] = nn(pick, x_ref[k]).astype(BF)
        gate_parts.append(
            jnp.sum(pick.astype(F32) * gate_row[:, k * rows : (k + 1) * rows], axis=1, keepdims=True)
        )
    gates = jnp.concatenate(gate_parts, axis=0)
    own = xg_ref[0]
    gate_pre = nn(own, wg_ref[0])
    up_pre = nn(own, wu_ref[0])
    raw_grad = dm_ref[0]
    sigmoid = 1.0 / (1.0 + jnp.exp(-gate_pre))
    swish = gate_pre * sigmoid
    active = swish * up_pre
    dgate = jnp.sum(active * raw_grad, axis=1, keepdims=True)
    gm_ref[0] = (gates * active).astype(BF)
    grad = gates * raw_grad
    da = (grad * up_pre * sigmoid * (1.0 + gate_pre * (1.0 - sigmoid))).astype(BF)
    db = (grad * swish).astype(BF)
    da_ref[0] = da
    db_ref[0] = db
    low = (nt(da, wg_ref[0]) + nt(db, wu_ref[0])).astype(BF)
    at = pl.multiple_of(step * slots, slots)
    for k in range(blocks):
        part = slice(k * slots, (k + 1) * slots)
        n_ref[k, pl.ds(at, slots), :] = low[part]
        dg_ref[0, k : k + 1, :] = jnp.sum(pick_ref[k, 0].astype(F32) * dgate[part], axis=0, keepdims=True)

    @pl.when(step == steps - 1)
    def _():
        for k in range(blocks):
            dn_ref[k] = nn(spread_ref[k], n_ref[k]).astype(BF)


def weights_kernel(own_ref, xg_ref, cg_ref, gm_ref, da_ref, db_ref, gu_keep, gu_send, d_keep, d_send):
    count = 2 * gu_keep.shape[0]
    width = xg_ref.shape[2] // count
    da, db, gm = da_ref[0], db_ref[0], gm_ref[0]
    for number in range(count):
        gu, down = (gu_send, d_send) if number % 2 else (gu_keep, d_keep)
        at = pl.multiple_of((own_ref[0] ^ number) * width, 128)
        rows = xg_ref[0, :, pl.ds(at, width)]
        gu[number // 2, 0, 0] = tn(rows, da).astype(BF)
        gu[number // 2, 0, 1] = tn(rows, db).astype(BF)
        down[number // 2, 0] = tn(gm, cg_ref[0, :, pl.ds(at, width)]).astype(BF)


def combine_kernel(gm_ref, wd_ref, spread_ref, out_ref, r_ref):
    blocks = out_ref.shape[0]
    slots = gm_ref.shape[1] // blocks
    step, steps = pl.program_id(0), pl.num_programs(0)
    low = nn(gm_ref[0], wd_ref[0]).astype(BF)
    at = pl.multiple_of(step * slots, slots)
    for k in range(blocks):
        r_ref[k, pl.ds(at, slots), :] = low[k * slots : (k + 1) * slots]

    @pl.when(step == steps - 1)
    def _():
        for k in range(blocks):
            out_ref[k] = nn(spread_ref[k], r_ref[k]).astype(BF)


def norm_forward(values, gain):
    norm_scale = lax.rsqrt(jnp.mean(values * values, axis=1, keepdims=True) + EPSILON)
    return (norm_scale, values * norm_scale * gain)


def norm_backward(values, norm_scale, gain, grad_normed):
    weighted = grad_normed * gain
    inner = jnp.mean(weighted * values, axis=1, keepdims=True)
    grad_values = norm_scale * weighted - values * (norm_scale * norm_scale * norm_scale) * inner
    grad_gain = jnp.sum(grad_normed * values * norm_scale, axis=0)
    return (grad_values, grad_gain)


def rotary_tables(length):
    half = HEAD_DIM // 2
    inverse = ROPE_BASE ** (-2.0 * np.arange(half) / HEAD_DIM)
    angles = np.arange(length)[:, None] * inverse[None, :]
    cosine, sine = np.cos(angles), np.sin(angles)
    return (
        np.concatenate([cosine, cosine, cosine, cosine], axis=1).astype(np.float32),
        np.concatenate([-sine, sine, -sine, sine], axis=1).astype(np.float32),
    )


def body(
    x_in,
    segments,
    chosen,
    out_grad,
    norm1_gain,
    w_query,
    w_key,
    w_value,
    w_out,
    norm2_gain,
    w_router,
    w_gate,
    w_up,
    w_down,
):
    tok_rows, full_width = x_in.shape
    h = HEAD_DIM
    q_width, kv_width = w_query.shape[1], w_key.shape[1]
    groups = q_width // kv_width
    experts_local, _, inner = w_gate.shape
    n_exp, n_dp = lax.axis_size("expert"), lax.axis_size("dp")
    total_experts = experts_local * n_exp
    top_count = chosen.shape[1]
    capacity = tok_rows * top_count * 25 // (16 * total_experts)
    place, side = lax.axis_index("expert"), lax.axis_index("tensor")
    half_width = full_width // lax.axis_size("tensor")
    row_start = place * tok_rows
    seq_length = segments.shape[0]
    half_rows = tok_rows // 2

    tables = [
        lax.dynamic_slice_in_dim(jnp.asarray(table), row_start, tok_rows)
        for table in rotary_tables(seq_length)
    ]
    cosine, sine = tables
    normed_one, query_rot, kv_own, scale_one = pl.pallas_call(
        project_kernel,
        name="project",
        out_shape=(
            jax.ShapeDtypeStruct((tok_rows, full_width), BF),
            jax.ShapeDtypeStruct((tok_rows, q_width), BF),
            jax.ShapeDtypeStruct((tok_rows, 2 * kv_width), BF),
            jax.ShapeDtypeStruct((tok_rows, 1), F32),
        ),
        compiler_params=params(32),
    )(x_in, norm1_gain[None], w_query, w_key, w_value, cosine, sine)
    kv_stack = jnp.stack([kv_own] + [fetch(kv_own, k) for k in range(1, n_exp)])
    order = (jnp.arange(n_exp) - place) % n_exp
    kv_all = jnp.take(kv_stack, order, axis=0).reshape(seq_length, -1)

    cot_in, chosen_in, kv_all = lax.optimization_barrier((out_grad, chosen, kv_all))
    cot_blocks = gather_blocks(cot_in, side)
    chosen_flip = jnp.where(side == 0, chosen_in, jnp.roll(chosen_in, half_rows, axis=0)).T
    chosen_blocks = jnp.stack([chosen_flip] + [fetch(chosen_flip, k) for k in range(1, n_exp)])
    expert_ids = jnp.arange(total_experts, dtype=jnp.int32)
    hot_all = jnp.any(chosen_blocks[:, :, None, :] == expert_ids[:, None], axis=1)
    hot_rows = hot_all.transpose(1, 0, 2).reshape(total_experts, n_exp * tok_rows).astype(F32)
    hot_local = lax.dynamic_slice_in_dim(hot_all, place * experts_local, experts_local, 1)
    token_row = jnp.arange(tok_rows, dtype=jnp.int32)
    before = (token_row[:, None] < token_row[None, :]).astype(BF)
    rank = jnp.einsum("kes,st->ket", hot_local.astype(BF), before, preferred_element_type=F32)
    slot_of = jnp.where(hot_local, rank.astype(jnp.int32), -1)
    slots = jnp.arange(capacity, dtype=jnp.int32)
    pick = (slot_of[:, :, None, :] == slots[:, None]).astype(BF)
    spread = pick.reshape(n_exp, experts_local * capacity, tok_rows).transpose(0, 2, 1)
    expert_slots = n_exp * capacity

    by_expert = lambda *tail: pl.BlockSpec((1,) + tail, lambda e, *_: (e,) + (0,) * len(tail))
    pick_spec = pl.BlockSpec((n_exp, 1, capacity, tok_rows), lambda e, *_: (0, e, 0, 0))
    blocks_shape = (n_exp, tok_rows, full_width)
    slots_shape = (n_exp, experts_local * capacity, full_width)
    cot_slots, raw_grad = pl.pallas_call(
        cotangent_kernel,
        name="cotangent",
        grid=(experts_local,),
        in_specs=[pick_spec, full(blocks_shape), by_expert(inner, full_width)],
        out_specs=(by_expert(expert_slots, full_width), by_expert(expert_slots, inner)),
        out_shape=(
            jax.ShapeDtypeStruct((experts_local, expert_slots, full_width), BF),
            jax.ShapeDtypeStruct((experts_local, expert_slots, inner), F32),
        ),
        compiler_params=params(40),
    )(pick, cot_blocks, w_down)

    positions = row_start + jnp.arange(tok_rows, dtype=jnp.int32)
    query_segments = lax.dynamic_slice_in_dim(segments, row_start, tok_rows)
    allowed = (query_segments[:, None] == segments[None, :]) & (
        positions[:, None] >= jnp.arange(seq_length, dtype=jnp.int32)[None, :]
    )
    bias = jnp.where(allowed, 0.0, MASKED).astype(F32)
    pair = 2 * h
    columns = lambda n: pl.BlockSpec((tok_rows, n), lambda i: (0, i))
    key_spec = pl.BlockSpec((seq_length, pair), lambda i: (0, i))
    value_spec = pl.BlockSpec((seq_length, pair), lambda i: (0, kv_width // pair + i))
    lse_spec = pl.BlockSpec((1, tok_rows, 2 * groups), lambda i: (i, 0, 0))
    steps = kv_width // pair
    attended, log_totals = pl.pallas_call(
        functools.partial(attend_kernel, groups),
        name="attend",
        grid=(steps,),
        in_specs=[columns(pair * groups), key_spec, value_spec, full((tok_rows, seq_length))],
        out_specs=(columns(pair * groups), lse_spec),
        out_shape=(
            jax.ShapeDtypeStruct((tok_rows, q_width), F32),
            jax.ShapeDtypeStruct((steps, tok_rows, 2 * groups), F32),
        ),
        compiler_params=params(32),
    )(query_rot, kv_all, kv_all, bias)
    attended_low = attended.astype(BF)
    head_low = nn(attended_low, w_out).astype(BF)
    inputs = x_in.astype(F32)
    hidden_one = inputs + head_low.astype(F32) + swap(head_low, "tensor").astype(F32)
    scale_two, normed_two = norm_forward(hidden_one, norm2_gain)
    normed_two = normed_two.astype(BF)

    token_blocks = gather_blocks(normed_two, side)
    low_slots = jax.ShapeDtypeStruct((experts_local, expert_slots, inner), BF)
    row_slots, gated, da, db, dgate_part, in_grad_part = pl.pallas_call(
        experts_kernel,
        name="experts",
        grid_spec=pltpu.PrefetchScalarGridSpec(
            num_scalar_prefetch=1,
            grid=(experts_local,),
            in_specs=[
                full(blocks_shape),
                full((total_experts, n_exp * tok_rows)),
                full((total_experts, full_width)),
                pick_spec,
                full((n_exp, tok_rows, experts_local * capacity)),
                by_expert(expert_slots, inner),
                by_expert(full_width, inner),
                by_expert(full_width, inner),
            ],
            out_specs=(
                by_expert(expert_slots, full_width),
                by_expert(expert_slots, inner),
                by_expert(expert_slots, inner),
                by_expert(expert_slots, inner),
                by_expert(n_exp, tok_rows),
                full(blocks_shape),
            ),
            scratch_shapes=[
                pltpu.VMEM((total_experts, n_exp * tok_rows), F32),
                pltpu.VMEM(slots_shape, BF),
            ],
        ),
        out_shape=(
            jax.ShapeDtypeStruct((experts_local, expert_slots, full_width), BF),
            low_slots,
            low_slots,
            low_slots,
            jax.ShapeDtypeStruct((experts_local, n_exp, tok_rows), F32),
            jax.ShapeDtypeStruct(blocks_shape, BF),
        ),
        compiler_params=params(52),
    )(place[None], token_blocks, hot_rows, w_router.T, pick, spread, raw_grad, w_gate, w_up)

    dgate_part = dgate_part.transpose(1, 0, 2)
    dgate_own = dgate_part + jnp.roll(swap(dgate_part, "tensor"), half_rows, axis=2)
    dgate_stack = jnp.stack([dgate_own[0]] + [deliver(dgate_own[k], k) for k in range(1, n_exp)])
    dgate = jnp.take(dgate_stack, (place - jnp.arange(n_exp)) % n_exp, axis=0)
    dgate = dgate.reshape(total_experts, tok_rows)
    dgate = jnp.where(side == 0, dgate, jnp.roll(dgate, half_rows, axis=1)).T
    hot_own = jnp.any(chosen[:, :, None] == expert_ids, axis=1)
    logits = jnp.where(hot_own, nn(normed_two, w_router), MASKED)
    raw = jnp.where(hot_own, jnp.exp(logits - jnp.max(logits, axis=-1, keepdims=True)), 0.0)
    gates_own = raw / jnp.sum(raw, axis=-1, keepdims=True)
    logit_grads = (
        gates_own * (dgate - jnp.sum(gates_own * dgate, axis=1, keepdims=True))
    ).astype(BF)
    half_sum = reduce_blocks(in_grad_part).astype(BF)
    half_other = swap(half_sum, "tensor")
    expert_grad = jnp.where(
        side == 0,
        jnp.concatenate([half_sum, half_other], axis=0),
        jnp.concatenate([half_other, half_sum], axis=0),
    ).astype(F32)

    slice_width = full_width // n_dp
    if slice_width % 128 == 0:
        expert_parts = []
        step_experts = experts_local // 2
        for first in (0, step_experts):
            count = step_experts if first == 0 else experts_local - step_experts
            some = lambda *tail: pl.BlockSpec(
                (1,) + tail, lambda e, *_: (first + e,) + (0,) * len(tail)
            )
            gu_shape = (n_dp // 2, count, 2, slice_width, inner)
            d_shape = (n_dp // 2, count, inner, slice_width)
            gu_spec = pl.BlockSpec((n_dp // 2, 1) + gu_shape[2:], lambda e, *_: (0, e, 0, 0, 0))
            d_spec = pl.BlockSpec((n_dp // 2, 1) + d_shape[2:], lambda e, *_: (0, e, 0, 0))
            gu_keep, gu_send, d_keep, d_send = pl.pallas_call(
                weights_kernel,
                name="weights",
                grid_spec=pltpu.PrefetchScalarGridSpec(
                    num_scalar_prefetch=1,
                    grid=(count,),
                    in_specs=[
                        some(expert_slots, full_width),
                        some(expert_slots, full_width),
                        some(expert_slots, inner),
                        some(expert_slots, inner),
                        some(expert_slots, inner),
                    ],
                    out_specs=(gu_spec, gu_spec, d_spec, d_spec),
                ),
                out_shape=(
                    jax.ShapeDtypeStruct(gu_shape, BF),
                    jax.ShapeDtypeStruct(gu_shape, BF),
                    jax.ShapeDtypeStruct(d_shape, BF),
                    jax.ShapeDtypeStruct(d_shape, BF),
                ),
                compiler_params=params(40),
            )(lax.axis_index("dp")[None], row_slots, cot_slots, gated, da, db)
            expert_parts.append((sum_places(gu_keep, gu_send), sum_places(d_keep, d_send)))
        gu_sum = jnp.concatenate([part[0] for part in expert_parts], axis=0)
        grad_gate, grad_up = gu_sum[:, 0], gu_sum[:, 1]
        grad_down = jnp.concatenate([part[1] for part in expert_parts], axis=0)
    else:
        sums = lambda spec, a, b: jnp.einsum(spec, a, b, preferred_element_type=F32).astype(BF)
        by_rows = lambda g: g.reshape(experts_local, n_dp, -1, inner).transpose(1, 0, 2, 3)
        grad_gate = sum_over_dp(by_rows(sums("esd,esf->edf", row_slots, da)))
        grad_up = sum_over_dp(by_rows(sums("esd,esf->edf", row_slots, db)))
        grad_down = sums("esf,esd->efd", gated, cot_slots)
        grad_down = sum_over_dp(
            grad_down.reshape(experts_local, inner, n_dp, -1).transpose(2, 0, 1, 3)
        )

    out_part = pl.pallas_call(
        combine_kernel,
        name="combine",
        grid=(experts_local,),
        in_specs=[
            by_expert(expert_slots, inner),
            by_expert(inner, full_width),
            full((n_exp, tok_rows, experts_local * capacity)),
        ],
        out_specs=full(blocks_shape),
        out_shape=jax.ShapeDtypeStruct(blocks_shape, BF),
        scratch_shapes=[pltpu.VMEM(slots_shape, BF)],
        compiler_params=params(40),
    )(gated, w_down, spread)
    out_mine = lax.dynamic_slice_in_dim(out_part, side * half_width, half_width, 2)
    out_else = lax.dynamic_slice_in_dim(out_part, (1 - side) * half_width, half_width, 2)
    out_got = jnp.roll(swap(out_else, "tensor"), half_rows, axis=1)
    out_sum = out_mine.astype(F32) + out_got.astype(F32)
    out_low = out_sum.astype(BF)
    mixture_half = out_sum[0]
    for k in range(1, n_exp):
        mixture_half = mixture_half + deliver(out_low[k], k).astype(F32)
    mixture_half = jnp.where(side == 0, mixture_half, jnp.roll(mixture_half, half_rows, axis=0))
    residual_half = lax.dynamic_slice_in_dim(hidden_one, side * half_width, half_width, 1)
    block_out = (residual_half + mixture_half).astype(BF)

    grad_router = tn(normed_two, logit_grads)
    out_cot = out_grad.astype(F32)
    normed_two_grad = nt(logit_grads, w_router) + expert_grad
    hidden_grad, gain_two_grad = norm_backward(hidden_one, scale_two, norm2_gain, normed_two_grad)
    hidden_grad = hidden_grad + out_cot
    branch_cot = hidden_grad.astype(BF)
    attended_grad = nt(branch_cot, w_out).astype(BF)
    grad_out = tn(branch_cot, attended_low)
    early = sum_over_tokens(
        jnp.concatenate([grad_out, grad_router, gain_two_grad[:, None]], axis=1).astype(BF)
    )

    kv_out = pl.BlockSpec((pair, seq_length), lambda i: (i, 0))
    query_grads, key_grads, value_grads = pl.pallas_call(
        functools.partial(attend_grad_kernel, groups),
        name="attend_grad",
        grid=(steps,),
        in_specs=[
            columns(pair * groups), key_spec, value_spec, columns(pair * groups),
            columns(pair * groups), lse_spec, full((tok_rows, seq_length)),
        ],
        out_specs=(columns(pair * groups), kv_out, kv_out),
        out_shape=(
            jax.ShapeDtypeStruct((tok_rows, q_width), F32),
            jax.ShapeDtypeStruct((kv_width, seq_length), BF),
            jax.ShapeDtypeStruct((kv_width, seq_length), BF),
        ),
        compiler_params=params(32),
    )(query_rot, kv_all, kv_all, attended_grad, attended, log_totals, bias)
    kv_grad = jnp.concatenate([key_grads, value_grads], axis=0)
    block_of = lambda k: lax.dynamic_slice_in_dim(
        kv_grad, ((place + k) % n_exp) * tok_rows, tok_rows, 1
    )
    kv_sum = block_of(0).astype(F32)
    for k in range(1, n_exp):
        kv_sum = kv_sum + deliver(block_of(k), k).astype(F32)
    kv_sum = kv_sum.T

    def turned_back(values):
        wide = values.reshape(tok_rows, -1, 2, h // 2)
        flipped = wide[:, :, ::-1].reshape(tok_rows, -1)
        count = values.shape[1] // (2 * h)
        return values * jnp.tile(cosine, (1, count)) - flipped * jnp.tile(sine, (1, count))

    query_grad = turned_back(query_grads).astype(BF)
    key_grad = turned_back(kv_sum[:, :kv_width]).astype(BF)
    value_grad = kv_sum[:, kv_width:].astype(BF)
    grad_query = tn(normed_one, query_grad)
    grad_key = tn(normed_one, key_grad)
    grad_value = tn(normed_one, value_grad)
    partial_low = (
        nt(query_grad, w_query) + nt(key_grad, w_key) + nt(value_grad, w_value)
    ).astype(BF)
    normed_one_grad = partial_low.astype(F32) + swap(partial_low, "tensor").astype(F32)
    input_part, gain_one_grad = norm_backward(inputs, scale_one, norm1_gain, normed_one_grad)
    input_grad = hidden_grad + input_part
    late_query = sum_over_tokens(grad_query.astype(BF))
    late = sum_over_tokens(
        jnp.concatenate([grad_key, grad_value, gain_one_grad[:, None]], axis=1).astype(BF)
    )
    return (
        block_out,
        input_grad,
        late[:, 2 * kv_width],
        late_query,
        late[:, :kv_width],
        late[:, kv_width : 2 * kv_width],
        early[:, :q_width].T,
        early[:, q_width + total_experts],
        early[:, q_width : q_width + total_experts],
        grad_gate,
        grad_up,
        grad_down,
    )


def solution(mesh):
    return jax.shard_map(
        body,
        mesh=mesh,
        in_specs=(
            P(("dp", "expert"), None),
            P("dp"),
            P(("dp", "expert"), None),
            P(("dp", "expert"), None),
            P(),
            P(None, "tensor"),
            P(None, "tensor"),
            P(None, "tensor"),
            P("tensor", None),
            P(),
            P(),
            P("expert", None, "tensor"),
            P("expert", None, "tensor"),
            P("expert", "tensor", None),
        ),
        out_specs=(
            P(("dp", "expert"), "tensor"),
            P(("dp", "expert"), None),
            P(("dp", "expert")),
            P(("dp", "expert"), "tensor"),
            P(("dp", "expert"), "tensor"),
            P(("dp", "expert"), "tensor"),
            P("tensor", ("dp", "expert")),
            P(("dp", "expert")),
            P(("dp", "expert"), None),
            P("expert", "dp", "tensor"),
            P("expert", "dp", "tensor"),
            P("expert", "tensor", "dp"),
        ),
        check_vma=False,
    )
```

time: 865 us -> 652 us (0.75)
  matrix products: 201 us -> 18.3 us
  Pallas kernels: 0 us -> 91.4 us
  waiting for transfers between devices: 323 us -> 255 us
  local copies, waits for them, and re-layouts: 141 us -> 95.9 us
  other arithmetic: 100 us -> 84.5 us
    dot_general x57 -> x13, matrix products: 198 us -> 18.3 us  [the longest x5 10.4 us: nt(): lax.dot_general(left, right, (((1,), (1,)), ((), ())), preferred_element_...]
    pallas_call x0 -> x8, Pallas kernels: none -> 91.4 us  [the longest x1 30.1 us: body(): pl.pallas_call(experts_kernel, name='experts', grid_spec=pltpu.PrefetchSc...]
    ppermute x12, waiting for transfers between devices: 57.8 us -> 1.83 us  [fetch(): lax.ppermute(values, 'expert', [(i, (i - offset) % count) for i in range(...]
    squeeze x14 -> x8, local copies, waits for them, and re-layouts: 27.9 us -> 4.98 us  [halve(): send = lax.dynamic_index_in_dim(pairs, 1 - own, 1, keepdims=False)]
    reshape x3 -> x1, local copies, waits for them, and re-layouts: 22.4 us -> 1.39 us  [turned_back(): flipped = wide[:, :, ::-1].reshape(tok_rows, -1)]
    unnamed x159 -> x186, local copies, waits for them, and re-layouts: 14.4 us -> 31.3 us
    convert_element_type x18 -> x15, other arithmetic: 33.4 us -> 18.7 us  [the longest x3 5.47 us: sum_over_tokens(): parts = halve(parts, 'dp', 1).astype(BF)]
    convert_element_type x4 -> x7, local copies, waits for them, and re-layouts: 19.4 us -> 6.91 us  [the longest x4 3.87 us: sum_places(): total = pairs[:, 0] + swap(pairs[:, 1].astype(BF), 'dp', bit).astype(F32)]
  transfers between devices with their start and end apart: 60 -> 62, of which waited for: 27 -> 21; matrix products, arithmetic and copies ran while one was open for 34% -> 23% of each run, Pallas kernels for 0% -> 9%
where the time goes in v2:
time: 652 us; the launch traced here: 641 us
  waiting for transfers between devices  255 us (39%)
  local copies, waits for them, and re-layouts  95.9 us (15%)
  starting transfers between devices  93.7 us (14%)
  Pallas kernels  91.4 us (14%)
  other arithmetic  84.5 us (13%)
  matrix products  18.3 us (3%)
    ppermute x29, waiting for transfers between devices, swap(): return lax.ppermute(values, axis, [(i, i ^ bit) for i in range(count)])  184 us
    ppermute x21, waiting for transfers between devices, deliver(): lax.ppermute(values, 'expert', [(i, (i + offset) % count) for i in range(...  69.7 us
    ppermute x21, starting transfers between devices, deliver(): lax.ppermute(values, 'expert', [(i, (i + offset) % count) for i in range(...  41 us
    unnamed x186, local copies, waits for them, and re-layouts  31.3 us
    pallas_call x1, Pallas kernels, body(): pl.pallas_call(experts_kernel, name='experts', grid_spec=pltpu.PrefetchSc...  30.1 us
    ppermute x29, starting transfers between devices, swap(): return lax.ppermute(values, axis, [(i, i ^ bit) for i in range(count)])  28.2 us
    ppermute x12, starting transfers between devices, fetch(): lax.ppermute(values, 'expert', [(i, (i - offset) % count) for i in range(...  24.5 us
    pallas_call x2, Pallas kernels, body(): pl.pallas_call(weights_kernel, name='weights', grid_spec=pltpu.PrefetchSc...  21.6 us
  transfers between devices with their start and end apart: 62, of which 21 were waited for; matrix products, arithmetic and copies ran while one was open for 23% of the time, Pallas kernels for 9%

profile of v2, /device:TPU:0, one launch (start us, length us, event | category | flops | bytes accessed | tf_op | source)
XLA Modules:
  0.0 641.5 jit_solution(2879029840908533811)
XLA Ops:
  40.3 6.2 collective-permute-start.12
  53.5 8.4 %attend.1 = (f32[256,768]{1,0:T(8,128)S(1)}, f32[2,256,6]{2,1,0:T(8,128)S(1)}) custom-call(bf16[256,768]{1,0:T(8,128)(2,1)S(1)} %copy-done.33, bf16[1024,512]{1,0:T(8,128)(2,1)S(1)} %bitcast_select_fusion.k_ref.v_ref, bf16[1024,512]{1,0:T(8,128)(2,1)S(1)} %bitcast_select_fusion.k_ref.v_ref, f32[256,1024]{1,0:T(8,128)S(1)} %copy-done.10), custom_call_target="tpu_custom_call" | custom-call | tf_op jit(solution)/shard_map/attend/pallas_call | solution.py:400
  98.5 5.8 collective-permute-done.16
  113.1 12.7 %cotangent.1 = (bf16[10,320,1536]{2,1,0:T(8,128)(2,1)}, f32[10,320,256]{2,1,0:T(8,128)S(1)}) custom-call(bf16[4,10,80,256]{3,2,1,0:T(8,128)(2,1)S(1)} %copy-done.4, bf16[4,256,1536]{2,1,0:T(8,128)(2,1)S(1)} %pad_maximum_fusion.3.cot_ref, bf16[10,256,1536]{2,1,0:T(8,128)(2,1)} %wd_ref.3), custom_call_target="tpu_custom_call" | custom-call | tf_op jit(solution)/shard_map/cotangent/pallas_call | solution.py:375
  129.9 7.9 %collective-permute-done.9 = bf16[128,1536]{1,0:T(8,128)(2,1)S(1)} collective-permute-done((bf16[128,1536]{1,0:T(8,128)(2,1)S(1)}, bf16[128,1536]{1,0:T(8,128)(2,1)S(1)}, u32[]{:S(2)}, u32[]{:S(2)}) %collective-permute-start.9) | collective-permute-done | bytes 393248 | tf_op jit(solution)/shard_map/ppermute | solution.py:22
  137.9 8.4 %collective-permute-done.7 = bf16[128,1536]{1,0:T(8,128)(2,1)S(1)} collective-permute-done((bf16[128,1536]{1,0:T(8,128)(2,1)S(1)}, bf16[128,1536]{1,0:T(8,128)(2,1)S(1)}, u32[]{:S(2)}, u32[]{:S(2)}) %collective-permute-start.7) | collective-permute-done | bytes 393248 | tf_op jit(solution)/shard_map/ppermute | solution.py:22
  146.3 5.3 collective-permute-done.5
  153.6 30.1 %experts.1 = (bf16[10,320,1536]{2,1,0:T(8,128)(2,1)}, bf16[10,320,256]{2,1,0:T(8,128)(2,1)S(1)}, bf16[10,320,256]{2,1,0:T(8,128)(2,1)}, bf16[10,320,256]{2,1,0:T...) custom-call(s32[1]{0:T(128)} %bitcast.6.place_ref, ...), custom_call_target="tpu_custom_call" | custom-call | tf_op jit(solution)/shard_map/experts/pallas_call | solution.py:421
  194.3 7.7 %combine.1 = bf16[4,256,1536]{2,1,0:T(8,128)(2,1)S(1)} custom-call(bf16[10,320,256]{2,1,0:T(8,128)(2,1)S(1)} %get-tuple-element.47.gm_ref, bf16[10,256,1536]{2,1,0:T(8,128)(2,1)S(1)} %copy-done.2, bf16[4,256,800]{2,1,0:T(8,128)(2,1)S(1)} %copy-done.3), custom_call_target="tpu_custom_call" | custom-call | tf_op jit(solution)/shard_map/combine/pallas_call | solution.py:532
  207.0 11.0 %weights.3 = (bf16[2,5,2,384,256]{4,3,2,1,0:T(8,128)(2,1)S(1)}, bf16[2,5,2,384,256]{4,3,2,1,0:T(8,128)(2,1)}, bf16[2,5,256,384]{3,2,1,0:T(8,128)(2,1)S(1)}, bf16[2,5,256,384]{3,2,1,0:T(8,128)(2,1)}) custom-call(s32[1]{0:T(128)} %bitcast.83.own_ref, bf16[10,320,1536]{2,1,0:T(8,128)(2,1)} %get-tuple-element.56.xg_ref, ...), custom_call_target="tpu_custom_call" | custom-call | tf_op jit(solution)/shard_map/weights/pallas_call | solution.py:495
  221.2 10.6 %weights.2 = (bf16[2,5,2,384,256]{4,3,2,1,0:T(8,128)(2,1)S(1)}, bf16[2,5,2,384,256]{4,3,2,1,0:T(8,128)(2,1)}, bf16[2,5,256,384]{3,2,1,0:T(8,128)(2,1)S(1)}, bf16[2,5,256,384]{3,2,1,0:T(8,128)(2,1)S(1)}) custom-call(s32[1]{0:T(128)} %bitcast.83.own_ref, bf16[10,320,1536]{2,1,0:T(8,128)(2,1)} %get-tuple-element.56.xg_ref, ...), custom_call_target="tpu_custom_call" | custom-call | tf_op jit(solution)/shard_map/weights/pallas_call | solution.py:495
  250.5 25.9 %collective-permute-done.33 = bf16[128,1536]{1,0:T(8,128)(2,1)} collective-permute-done((bf16[128,1536]{1,0:T(8,128)(2,1)}, bf16[128,1536]{1,0:T(8,128)(2,1)}, u32[]{:S(2)}, u32[]{:S(2)}) %collective-permute-start.33) | collective-permute-done | bytes 393248 | tf_op jit(solution)/shard_map/ppermute | solution.py:22
  284.7 5.7 collective-permute-done.34
  299.0 9.3 %attend_grad.1 = (f32[256,768]{1,0:T(8,128)S(1)}, bf16[256,1024]{1,0:T(8,128)(2,1)S(1)}, bf16[256,1024]{1,0:T(8,128)(2,1)S(1)}) custom-call(bf16[256,768]{1,0:T(8,128)(2,1)S(1)} %copy-done.34, bf16[1024,512]{1,0:T(8,128)(2,1)S(1)} %bitcast_select_fusion.k_ref.v_ref, bf16[1024,512]{1,0:T(8,128)(2,1)S(1)} %bitcast_select_fusion.k_ref.v_ref, ...), custom_call_target="tpu_custom_call" | custom-call | tf_op jit(solution)/shard_map/attend_grad/pallas_call | solution.py:571
  364.5 25.5 %collective-permute-done.21 = bf16[256,768]{1,0:T(8,128)(2,1)} collective-permute-done((bf16[256,768]{1,0:T(8,128)(2,1)}, bf16[256,768]{1,0:T(8,128)(2,1)}, u32[]{:S(2)}, u32[]{:S(2)}) %collective-permute-start.21) | collective-permute-done | bytes 393248 | tf_op jit(solution)/shard_map/ppermute | solution.py:32
  402.1 9.8 %collective-permute-done.38 = bf16[256,1536]{1,0:T(8,128)(2,1)S(1)} collective-permute-done((bf16[256,1536]{1,0:T(8,128)(2,1)S(1)}, bf16[256,1536]{1,0:T(8,128)(2,1)S(1)}, u32[]{:S(2)}, u32[]{:S(2)}) %collective-permute-start.38) | collective-permute-done | bytes 786464 | tf_op jit(solution)/shard_map/ppermute | solution.py:22
  431.9 15.8 %collective-permute-done.46 = bf16[2,96,768]{2,1,0:T(8,128)(2,1)} collective-permute-done((bf16[2,96,768]{2,1,0:T(8,128)(2,1)S(1)}, bf16[2,96,768]{2,1,0:T(8,128)(2,1)}, u32[]{:S(2)}, u32[]{:S(2)}) %collective-permute-start.46) | collective-permute-done | bytes 294944 | tf_op jit(solution)/shard_map/ppermute | solution.py:32
  447.6 13.4 %collective-permute-start.50 = (bf16[2,96,809]{2,1,0:T(8,128)(2,1)S(1)}, bf16[2,96,809]{2,1,0:T(8,128)(2,1)S(1)}, u32[]{:S(2)}, u32[]{:S(2)}) collective-permute-start(bf16[2,96,809]{2,1,0:T(8,128)(2,1)S(1)} %get-tuple-element.176), channel_id=1, source_target_pairs={{0,2},{2,4},{4,6},{6,0},{1,3},{3,5},{5,7},{7,1},{8,10},{10,12},{12... | collective-permute-start | bytes 931976 | tf_op jit(solution)/shard_map/ppermute | solution.py:32
  464.1 10.1 %collective-permute-done.51 = bf16[2,96,809]{2,1,0:T(8,128)(2,1)S(1)} collective-permute-done((bf16[2,96,809]{2,1,0:T(8,128)(2,1)S(1)}, bf16[2,96,809]{2,1,0:T(8,128)(2,1)S(1)}, u32[]{:S(2)}, u32[]{:S(2)}) %collective-permute-start.51) | collective-permute-done | bytes 310688 | tf_op jit(solution)/shard_map/ppermute | solution.py:32
  476.5 33.8 %collective-permute-done.48 = bf16[1,96,768]{2,1,0:T(8,128)(2,1)S(1)} collective-permute-done((bf16[1,96,768]{2,1,0:T(8,128)(2,1)S(1)}, bf16[1,96,768]{2,1,0:T(8,128)(2,1)S(1)}, u32[]{:S(2)}, u32[]{:S(2)}) %collective-permute-start.48) | collective-permute-done | bytes 147488 | tf_op jit(solution)/shard_map/ppermute | solution.py:22
  523.8 6.5 %collective-permute-start.41 = (bf16[2,96,513]{2,1,0:T(8,128)(2,1)S(1)}, bf16[2,96,513]{2,1,0:T(8,128)(2,1)}, u32[]{:S(2)}, u32[]{:S(2)}) collective-permute-start(bf16[2,96,513]{2,1,0:T(8,128)(2,1)S(1)} %get-tuple-element.187), channel_id=1, source_target_pairs={{0,4},{2,6},{4,0},{6,2},{1,5},{3,7},{5,1},{7,3},{8,12},{10,14},{12... | collective-permute-start | bytes 590984 | tf_op jit(solution)/shard_map/ppermute | solution.py:32
  544.3 8.2 %collective-permute-done.41 = bf16[2,96,513]{2,1,0:T(8,128)(2,1)} collective-permute-done((bf16[2,96,513]{2,1,0:T(8,128)(2,1)S(1)}, bf16[2,96,513]{2,1,0:T(8,128)(2,1)}, u32[]{:S(2)}, u32[]{:S(2)}) %collective-permute-start.41) | collective-permute-done | bytes 197024 | tf_op jit(solution)/shard_map/ppermute | solution.py:32
  557.5 68.2 %collective-permute-done.43 = bf16[1,96,513]{2,1,0:T(8,128)(2,1)S(1)} collective-permute-done((bf16[1,96,513]{2,1,0:T(8,128)(2,1)S(1)}, bf16[1,96,513]{2,1,0:T(8,128)(2,1)S(1)}, u32[]{:S(2)}, u32[]{:S(2)}) %collective-permute-start.43) | collective-permute-done | bytes 98528 | tf_op jit(solution)/shard_map/ppermute | solution.py:22
  633.6 7.4 %fusion.2 = (f32[10,384,256]{2,1,0:T(8,128)}, f32[10,384,256]{2,1,0:T(8,128)}) fusion(f32[5,2,384,256]{3,2,1,0:T(8,128)} %fusion.4, f32[5,2,384,256]{3,2,1,0:T(8,128)} %fusion.6), kind=kLoop, calls=%fused_computation.9 | loop fusion | flops 1966080 | bytes 15728640 | tf_op jit(solution)/shard_map/squeeze | solution.py:520
  (445 shorter events, 285.5 us)
Async XLA Ops:
  90.6 35.2 %collective-permute-start.8 = (bf16[128,1536]{1,0:T(8,128)(2,1)S(1)}, bf16[128,1536]{1,0:T(8,128)(2,1)S(1)}, u32[]{:S(2)}, u32[]{:S(2)}) collective-permute-start(bf16[128,1536]{1,0:T(8,128)(2,1)S(1)} %get-tuple-element.193), channel_id=1, source_target_pairs={{0,2},{2,4},{4,6},{6,0},{1,3},{3,5},{5,7},{7,1},{8,10},{10,12},{12... | collective-permute-start | bytes 1179656 | tf_op jit(solution)/shard_map/ppermute | solution.py:27
  93.1 34.3 %collective-permute-start.6 = (bf16[128,1536]{1,0:T(8,128)(2,1)S(1)}, bf16[128,1536]{1,0:T(8,128)(2,1)S(1)}, u32[]{:S(2)}, u32[]{:S(2)}) collective-permute-start(bf16[128,1536]{1,0:T(8,128)(2,1)S(1)} %get-tuple-element.193), channel_id=1, source_target_pairs={{0,4},{2,6},{4,0},{6,2},{1,5},{3,7},{5,1},{7,3},{8,12},{10,14},{12... | collective-permute-start | bytes 1179656 | tf_op jit(solution)/shard_map/ppermute | solution.py:27
  95.9 32.4 %collective-permute-start.4 = (bf16[128,1536]{1,0:T(8,128)(2,1)S(1)}, bf16[128,1536]{1,0:T(8,128)(2,1)S(1)}, u32[]{:S(2)}, u32[]{:S(2)}) collective-permute-start(bf16[128,1536]{1,0:T(8,128)(2,1)S(1)} %get-tuple-element.193), channel_id=1, source_target_pairs={{0,6},{2,0},{4,2},{6,4},{1,7},{3,1},{5,3},{7,5},{8,14},{10,8},{12,... | collective-permute-start | bytes 1179656 | tf_op jit(solution)/shard_map/ppermute | solution.py:27
  187.8 54.8 %collective-permute-start.27 = (bf16[128,1536]{1,0:T(8,128)(2,1)}, bf16[128,1536]{1,0:T(8,128)(2,1)}, u32[]{:S(2)}, u32[]{:S(2)}) collective-permute-start(bf16[128,1536]{1,0:T(8,128)(2,1)} %get-tuple-element.167), channel_id=1, source_target_pairs={{0,1},{1,0},{2,3},{3,2},{4,5},{5,4},{6,7},{7,6},{8,9},{9,8},{10,11... | collective-permute-start | bytes 1179656 | tf_op jit(solution)/shard_map/ppermute | solution.py:22
  188.3 54.3 %collective-permute-start.31 = (bf16[128,1536]{1,0:T(8,128)(2,1)}, bf16[128,1536]{1,0:T(8,128)(2,1)}, u32[]{:S(2)}, u32[]{:S(2)}) collective-permute-start(bf16[128,1536]{1,0:T(8,128)(2,1)} %get-tuple-element.169), channel_id=1, source_target_pairs={{0,1},{1,0},{2,3},{3,2},{4,5},{5,4},{6,7},{7,6},{8,9},{9,8},{10,11... | collective-permute-start | bytes 1179656 | tf_op jit(solution)/shard_map/ppermute | solution.py:22
  189.8 52.8 %collective-permute-start.29 = (bf16[128,1536]{1,0:T(8,128)(2,1)}, bf16[128,1536]{1,0:T(8,128)(2,1)}, u32[]{:S(2)}, u32[]{:S(2)}) collective-permute-start(bf16[128,1536]{1,0:T(8,128)(2,1)} %get-tuple-element.170), channel_id=1, source_target_pairs={{0,1},{1,0},{2,3},{3,2},{4,5},{5,4},{6,7},{7,6},{8,9},{9,8},{10,11... | collective-permute-start | bytes 1179656 | tf_op jit(solution)/shard_map/ppermute | solution.py:22
  202.1 34.3 %collective-permute-start.25 = (f32[10,256]{1,0:T(8,128)S(1)}, f32[10,256]{1,0:T(8,128)S(1)}, u32[]{:S(2)}, u32[]{:S(2)}) collective-permute-start(f32[10,256]{1,0:T(8,128)S(1)} %bitcast.275), channel_id=1, source_target_pairs={{0,4},{2,6},{4,0},{6,2},{1,5},{3,7},{5,1},{7,3},{8,12},{10,14},{12... | collective-permute-start | bytes 30728 | tf_op jit(solution)/shard_map/ppermute | solution.py:32
  204.1 33.8 %collective-permute-start.24 = (f32[10,256]{1,0:T(8,128)S(1)}, f32[10,256]{1,0:T(8,128)S(1)}, u32[]{:S(2)}, u32[]{:S(2)}) collective-permute-start(f32[10,256]{1,0:T(8,128)S(1)} %bitcast.274), channel_id=1, source_target_pairs={{0,2},{2,4},{4,6},{6,0},{1,3},{3,5},{5,7},{7,1},{8,10},{10,12},{12... | collective-permute-start | bytes 30728 | tf_op jit(solution)/shard_map/ppermute | solution.py:32
  236.3 110.9 %collective-permute-start.19 = (bf16[4,256,768]{2,1,0:T(8,128)(2,1)}, bf16[4,256,768]{2,1,0:T(8,128)(2,1)}, u32[]{:S(2)}, u32[]{:S(2)}) collective-permute-start(bf16[4,256,768]{2,1,0:T(8,128)(2,1)} %constant_dynamic-slice_fusion.6), channel_id=1, source_target_pairs={{0,1},{1,0},{2,3},{3,2},{4,5},{5,4},{6,7},{7,6},{8,9},{9,8},{10,11... | collective-permute-start | bytes 4718600 | tf_op jit(solution)/shard_map/ppermute | solution.py:22
  237.9 38.5 %collective-permute-start.33 = (bf16[128,1536]{1,0:T(8,128)(2,1)}, bf16[128,1536]{1,0:T(8,128)(2,1)}, u32[]{:S(2)}, u32[]{:S(2)}) collective-permute-start(bf16[128,1536]{1,0:T(8,128)(2,1)} %get-tuple-element.168), channel_id=1, source_target_pairs={{0,1},{1,0},{2,3},{3,2},{4,5},{5,4},{6,7},{7,6},{8,9},{9,8},{10,11... | collective-permute-start | bytes 1179656 | tf_op jit(solution)/shard_map/ppermute | solution.py:22
  244.5 31.8 %collective-permute-start.32 = (bf16[128,1536]{1,0:T(8,128)(2,1)S(1)}, bf16[128,1536]{1,0:T(8,128)(2,1)S(1)}, u32[]{:S(2)}, u32[]{:S(2)}) collective-permute-start(bf16[128,1536]{1,0:T(8,128)(2,1)S(1)} %get-tuple-element.165), channel_id=1, source_target_pairs={{0,2},{2,4},{4,6},{6,0},{1,3},{3,5},{5,7},{7,1},{8,10},{10,12},{12... | collective-permute-start | bytes 1179656 | tf_op jit(solution)/shard_map/ppermute | solution.py:32
  276.4 116.0 %collective-permute-start.60 = (bf16[2,5,256,384]{3,2,1,0:T(8,128)(2,1)}, bf16[2,5,256,384]{3,2,1,0:T(8,128)(2,1)}, u32[]{:S(2)}, u32[]{:S(2)}) collective-permute-start(bf16[2,5,256,384]{3,2,1,0:T(8,128)(2,1)} %get-tuple-element.67), channel_id=1, source_target_pairs={{0,8},{8,0},{16,24},{24,16},{1,9},{9,1},{17,25},{25,17},{2,10},{10... | collective-permute-start | bytes 5898248 | tf_op jit(solution)/shard_map/ppermute | solution.py:22
  332.7 65.8 %collective-permute-start.58 = (bf16[2,5,256,384]{3,2,1,0:T(8,128)(2,1)S(1)}, bf16[2,5,256,384]{3,2,1,0:T(8,128)(2,1)}, u32[]{:S(2)}, u32[]{:S(2)}) collective-permute-start(bf16[2,5,256,384]{3,2,1,0:T(8,128)(2,1)S(1)} %copy-done.40), channel_id=1, source_target_pairs={{0,8},{8,0},{16,24},{24,16},{1,9},{9,1},{17,25},{25,17},{2,10},{10... | collective-permute-start | bytes 5898248 | tf_op jit(solution)/shard_map/ppermute | solution.py:22
  352.7 37.3 %collective-permute-start.21 = (bf16[256,768]{1,0:T(8,128)(2,1)}, bf16[256,768]{1,0:T(8,128)(2,1)}, u32[]{:S(2)}, u32[]{:S(2)}) collective-permute-start(bf16[256,768]{1,0:T(8,128)(2,1)} %get-tuple-element.173), channel_id=1, source_target_pairs={{0,4},{2,6},{4,0},{6,2},{1,5},{3,7},{5,1},{7,3},{8,12},{10,14},{12... | collective-permute-start | bytes 1179656 | tf_op jit(solution)/shard_map/ppermute | solution.py:32
  355.7 34.3 %collective-permute-start.20 = (bf16[256,768]{1,0:T(8,128)(2,1)}, bf16[256,768]{1,0:T(8,128)(2,1)}, u32[]{:S(2)}, u32[]{:S(2)}) collective-permute-start(bf16[256,768]{1,0:T(8,128)(2,1)} %get-tuple-element.171), channel_id=1, source_target_pairs={{0,2},{2,4},{4,6},{6,0},{1,3},{3,5},{5,7},{7,1},{8,10},{10,12},{12... | collective-permute-start | bytes 1179656 | tf_op jit(solution)/shard_map/ppermute | solution.py:32
  364.4 165.8 %collective-permute-start.56 = (bf16[2,5,2,384,256]{4,3,2,1,0:T(8,128)(2,1)}, bf16[2,5,2,384,256]{4,3,2,1,0:T(8,128)(2,1)}, u32[]{:S(2)}, u32[]{:S(2)}) collective-permute-start(bf16[2,5,2,384,256]{4,3,2,1,0:T(8,128)(2,1)} %get-tuple-element.63), channel_id=1, source_target_pairs={{0,8},{8,0},{16,24},{24,16},{1,9},{9,1},{17,25},{25,17},{2,10},{10... | collective-permute-start | bytes 11796488 | tf_op jit(solution)/shard_map/ppermute | solution.py:22
  390.0 146.1 %collective-permute-start.54 = (bf16[2,5,2,384,256]{4,3,2,1,0:T(8,128)(2,1)}, bf16[2,5,2,384,256]{4,3,2,1,0:T(8,128)(2,1)}, u32[]{:S(2)}, u32[]{:S(2)}) collective-permute-start(bf16[2,5,2,384,256]{4,3,2,1,0:T(8,128)(2,1)} %get-tuple-element.61), channel_id=1, source_target_pairs={{0,8},{8,0},{16,24},{24,16},{1,9},{9,1},{17,25},{25,17},{2,10},{10... | collective-permute-start | bytes 11796488 | tf_op jit(solution)/shard_map/ppermute | solution.py:22
  429.5 33.0 %collective-permute-start.52 = (bf16[2,96,809]{2,1,0:T(8,128)(2,1)S(1)}, bf16[2,96,809]{2,1,0:T(8,128)(2,1)S(1)}, u32[]{:S(2)}, u32[]{:S(2)}) collective-permute-start(bf16[2,96,809]{2,1,0:T(8,128)(2,1)S(1)} %get-tuple-element.177), channel_id=1, source_target_pairs={{0,6},{2,0},{4,2},{6,4},{1,7},{3,1},{5,3},{7,5},{8,14},{10,8},{12,... | collective-permute-start | bytes 931976 | tf_op jit(solution)/shard_map/ppermute | solution.py:32
  462.5 55.4 %collective-permute-start.61 = (bf16[1,5,256,384]{3,2,1,0:T(8,128)(2,1)}, bf16[1,5,256,384]{3,2,1,0:T(8,128)(2,1)S(1)}, u32[]{:S(2)}, u32[]{:S(2)}) collective-permute-start(bf16[1,5,256,384]{3,2,1,0:T(8,128)(2,1)} %fusion.32), channel_id=1, source_target_pairs={{0,16},{8,24},{16,0},{24,8},{1,17},{9,25},{17,1},{25,9},{2,18},{10... | collective-permute-start | bytes 2949128 | tf_op jit(solution)/shard_map/ppermute | solution.py:22
  474.2 66.7 %collective-permute-start.59 = (bf16[1,5,256,384]{3,2,1,0:T(8,128)(2,1)}, bf16[1,5,256,384]{3,2,1,0:T(8,128)(2,1)}, u32[]{:S(2)}, u32[]{:S(2)}) collective-permute-start(bf16[1,5,256,384]{3,2,1,0:T(8,128)(2,1)} %fusion.31), channel_id=1, source_target_pairs={{0,16},{8,24},{16,0},{24,8},{1,17},{9,25},{17,1},{25,9},{2,18},{10... | collective-permute-start | bytes 2949128 | tf_op jit(solution)/shard_map/ppermute | solution.py:22
  475.8 34.5 %collective-permute-start.48 = (bf16[1,96,768]{2,1,0:T(8,128)(2,1)S(1)}, bf16[1,96,768]{2,1,0:T(8,128)(2,1)S(1)}, u32[]{:S(2)}, u32[]{:S(2)}) collective-permute-start(bf16[1,96,768]{2,1,0:T(8,128)(2,1)S(1)} %constant_dynamic-slice_fusion.1), channel_id=1, source_target_pairs={{0,16},{8,24},{16,0},{24,8},{1,17},{9,25},{17,1},{25,9},{2,18},{10... | collective-permute-start | bytes 442376 | tf_op jit(solution)/shard_map/ppermute | solution.py:22
  536.1 91.0 %collective-permute-start.57 = (bf16[1,5,2,384,256]{4,3,2,1,0:T(8,128)(2,1)}, bf16[1,5,2,384,256]{4,3,2,1,0:T(8,128)(2,1)}, u32[]{:S(2)}, u32[]{:S(2)}) collective-permute-start(bf16[1,5,2,384,256]{4,3,2,1,0:T(8,128)(2,1)} %fusion.12), channel_id=1, source_target_pairs={{0,16},{8,24},{16,0},{24,8},{1,17},{9,25},{17,1},{25,9},{2,18},{10... | collective-permute-start | bytes 5898248 | tf_op jit(solution)/shard_map/ppermute | solution.py:22
  541.0 90.2 %collective-permute-start.55 = (bf16[1,5,2,384,256]{4,3,2,1,0:T(8,128)(2,1)S(1)}, bf16[1,5,2,384,256]{4,3,2,1,0:T(8,128)(2,1)S(1)}, u32[]{:S(2)}, u32[]{:S(2)}) collective-permute-start(bf16[1,5,2,384,256]{4,3,2,1,0:T(8,128)(2,1)S(1)} %fusion.11), channel_id=1, source_target_pairs={{0,16},{8,24},{16,0},{24,8},{1,17},{9,25},{17,1},{25,9},{2,18},{10... | collective-permute-start | bytes 5898248 | tf_op jit(solution)/shard_map/ppermute | solution.py:22
  553.7 72.1 %collective-permute-start.43 = (bf16[1,96,513]{2,1,0:T(8,128)(2,1)S(1)}, bf16[1,96,513]{2,1,0:T(8,128)(2,1)S(1)}, u32[]{:S(2)}, u32[]{:S(2)}) collective-permute-start(bf16[1,96,513]{2,1,0:T(8,128)(2,1)S(1)} %constant_dynamic-slice_fusion.2), channel_id=1, source_target_pairs={{0,16},{8,24},{16,0},{24,8},{1,17},{9,25},{17,1},{25,9},{2,18},{10... | collective-permute-start | bytes 295496 | tf_op jit(solution)/shard_map/ppermute | solution.py:22
  (128 other events, 1491.0 us)
